TPU v7x, 256 devices: a whole 4x4x8 slice. The times are simulated.
256 devices in a mesh: space: 32 (over z_lo, y, core), fac: 8 (over z_hi, x).
Axes of the slice: x: 4, y: 4, z: 8 (z_hi: 2, z_lo: 4; z = z_hi * 4 + z_lo), core: 2. Of those that a mesh axis runs over, the one named last changes fastest.
Arguments:
- activations: bfloat16 [8, 64, 16, 16, 128], P('fac', 'space'), may hold values from -60 to 60
- out_grad: bfloat16 [8, 64, 16, 16, 128], P('fac', 'space'), may hold values from -60 to 60
- kernel: bfloat16 [27, 128, 128], replicated, may hold values from -0.109375 to 0.109375
Outputs:
- in_grad: bfloat16 [8, 64, 16, 16, 128], P('fac', 'space')
- update: float32 [27, 128, 128], P(None, 'fac')
All inputs are finite; a program needn't handle non-finite values.
Results may differ from a plain program's by a relative error of at most 0.0014.
Values may be sent and summed in bfloat16 or wider, within the bound.
No kernel may reach another device: no remote copies, remote signals or barrier semaphores. Data moves between devices by JAX's collectives and lax.ppermute only.
A program may use at most 128 MiB of HBM per device.

v0:
```python
import math

import jax
import jax.numpy as jnp
from jax import lax
from jax.sharding import PartitionSpec as P

damping = 0.1
clip_rate = 0.05


def with_halo(cells, sides, width):
    for axis, dim in sides:
        count = lax.axis_size(axis)
        ends = count - 1
        head = lax.slice_in_dim(cells, 0, width, axis=dim)
        tail = lax.slice_in_dim(cells, cells.shape[dim] - width, cells.shape[dim], axis=dim)
        cells = jnp.concatenate(
            [
                lax.ppermute(tail, axis, [(i, (i + 1) % count) for i in range(ends)]),
                cells,
                lax.ppermute(head, axis, [((i + 1) % count, i) for i in range(ends)]),
            ],
            axis=dim,
        )
    return cells


def offsets():
    return [(a, b, c) for a in (-1, 0, 1) for b in (-1, 0, 1) for c in (-1, 0, 1)]


def window(padded, shift, extent):
    return padded[
        1 + shift[0] : 1 + shift[0] + extent[0],
        1 + shift[1] : 1 + shift[1] + extent[1],
        1 + shift[2] : 1 + shift[2] + extent[2],
    ]


def local_stats(padded_in, rows_cot, extent, groups):
    cells = rows_cot.shape[0]
    width = padded_in.shape[-1] // groups
    gram_list = []
    grad_list = []
    for block_index in range(groups):
        lower = block_index * width
        pieces = [
            window(padded_in, shift, extent)[..., lower : lower + width].reshape(cells, width)
            for shift in offsets()
        ]
        patch = jnp.concatenate(pieces, axis=1)
        gram_list.append(jnp.dot(patch.T, patch, preferred_element_type=jnp.float32))
        grad_list.append(jnp.dot(patch.T, rows_cot, preferred_element_type=jnp.float32))
    grads = jnp.stack(grad_list)
    return (jnp.stack(gram_list), grads)


def on_device(activations, out_grad, kernel):
    inputs = activations[0]
    cotangent = out_grad[0]
    size_x, size_y, size_z, channels = inputs.shape
    extent = (size_x, size_y, size_z)
    cells = size_x * size_y * size_z
    groups = lax.axis_size("fac")
    width = channels // groups
    stacked = jnp.concatenate([inputs, cotangent], axis=3)
    rimmed = with_halo(stacked, (("space", 0),), 1)
    padded = jnp.pad(rimmed, ((0, 0), (1, 1), (1, 1), (0, 0)))
    padded_in = padded[..., :channels]
    padded_cot = padded[..., channels:]
    rows_cot = cotangent.reshape(cells, channels)
    cot_gram = jnp.dot(rows_cot.T, rows_cot, preferred_element_type=jnp.float32)
    in_grad = jnp.zeros((cells, channels), jnp.float32)
    for tap_index, shift in enumerate(offsets()):
        back = (-shift[0], -shift[1], -shift[2])
        rows = window(padded_cot, back, extent).reshape(cells, channels)
        in_grad = in_grad + jnp.dot(rows, kernel[tap_index].T, preferred_element_type=jnp.float32)
    in_grad = in_grad.astype(jnp.bfloat16).reshape(activations.shape)
    cot_total = lax.psum(cot_gram, ("space", "fac"))
    grams, grads = local_stats(padded_in, rows_cot, extent, groups)
    summed = lax.psum((grams, grads), "space")
    owned = (
        lax.psum_scatter(summed[0], "fac", scatter_dimension=0, tiled=True),
        lax.psum_scatter(summed[1], "fac", scatter_dimension=0, tiled=True),
    )
    gram_block = owned[0][0]
    grad_block = owned[1][0]
    count = float(cells * lax.axis_size("space") * groups)
    order = gram_block.shape[0]
    right_mat = cot_total / count + damping * jnp.eye(channels, dtype=jnp.float32)
    right_chol = jnp.linalg.cholesky(right_mat)
    left_mat = gram_block / count + damping * jnp.eye(order, dtype=jnp.float32)
    left_chol = jnp.linalg.cholesky(left_mat)
    scaled = grad_block / math.sqrt(count)
    half = jax.scipy.linalg.cho_solve((left_chol, True), scaled)
    raw = jax.scipy.linalg.cho_solve((right_chol, True), half.T).T
    total = lax.psum(jnp.sum(raw * scaled), "fac")
    factor = jnp.sqrt(clip_rate * kernel.size / total)
    update = raw.reshape(27, width, channels) * factor
    return (in_grad, update)


def solution(mesh):
    placed = (P("fac", "space", None, None, None), P("fac", "space", None, None, None), P())
    return jax.shard_map(
        on_device,
        mesh=mesh,
        in_specs=placed,
        out_specs=(P("fac", "space", None, None, None), P(None, "fac", None)),
        check_vma=False,
    )
```

profile of v0, /device:TPU:1, one launch (start us, length us, event | category | flops | bytes accessed | tf_op | source)
XLA Modules:
  0.0 791.2 jit_solution(12100450884241944340)
XLA Ops:
  11.0 4.6 collective-permute-start
  46.3 3.6 concatenate.80
  50.9 3.4 concatenate.81
  55.3 3.3 concatenate.82
  59.6 3.4 concatenate.83
  64.0 4.2 concatenate.84
  70.3 4.2 concatenate.85
  76.6 4.2 concatenate.86
  82.9 4.2 concatenate.87
  101.0 208.4 %all-reduce.8.cloned.1.call-done = f32[128,128]{1,0:T(8,128)} async-done(((f32[128,128]{1,0:T(8,128)}), f32[128,128]{1,0:T(8,128)}) %all-reduce.8.cloned.1.call-update) | async-done | bytes 65552 | tf_op jit(solution)/shard_map/psum | solution.py:80
  311.3 11.7 %cholesky.100 = f32[128,128]{1,0:T(8,128)S(1)} custom-call(f32[128,128]{1,0:T(8,128)S(1)} %fusion.73), custom_call_target="Cholesky" | custom-call | tf_op jit(solution)/shard_map/jit(cholesky)/cholesky | solution.py:92
  324.3 10.4 %custom-call.44 = f32[1,128,128]{1,2,0:T(8,128)} custom-call(f32[1,128,128]{2,1,0:T(8,128)S(1)} %fusion.62), custom_call_target="InvertDiagBlocksLowerTriangular" | custom-call | tf_op jit(solution)/shard_map/jit(_cho_solve)/triangular_solve | solution.py:97
  341.2 9.8 %reduce-scatter.3.cloned.1.call-done = f32[1,432,432]{2,1,0:T(8,128)} async-done(((f32[8,432,432]{2,1,0:T(8,128)}), f32[1,432,432]{2,1,0:T(8,128)}) %reduce-scatter.3.cloned.1.call-update) | async-done | bytes 746512 | tf_op jit(solution)/shard_map/reduce_scatter | solution.py:84
  352.6 268.6 %all-reduce.10.cloned.1.call-done = (f32[1,432,432]{2,1,0:T(8,128)}, f32[1,432,128]{2,1,0:T(8,128)}) async-done(((f32[1,432,432]{2,1,0:T(8,128)}, f32[1,432,128]{2,1,0:T(8,128)}), (f32[1,432,432]{2,1,0:T(8,128)}, f32[1,432,128]{2,1,0:T(8,128)})) %all-reduce.10.cloned.1.call-update) | async-done | bytes 967696 | tf_op jit(solution)/shard_map/psum | solution.py:82
  624.1 11.9 %cholesky.109 = f32[128,128]{1,0:T(8,128)S(1)} custom-call(f32[128,128]{1,0:T(8,128)S(1)} %cholesky.264), custom_call_target="Cholesky" | custom-call | tf_op jit(solution)/shard_map/jit(cholesky)/cholesky | solution.py:94
  636.8 9.8 %custom-call.45 = f32[1,128,128]{1,2,0:T(8,128)S(1)} custom-call(f32[1,128,128]{2,1,0:T(8,128)S(1)} %get-tuple-element.273), custom_call_target="InvertDiagBlocksLowerTriangular" | custom-call | tf_op jit(solution)/shard_map/jit(cholesky)/cholesky | solution.py:94
  649.2 11.7 %cholesky.212 = f32[128,128]{1,0:T(8,128)S(1)} custom-call(f32[128,128]{1,0:T(8,128)S(1)} %cholesky.268), custom_call_target="Cholesky" | custom-call | tf_op jit(solution)/shard_map/jit(cholesky)/cholesky | solution.py:94
  661.6 9.8 %custom-call.46 = f32[1,128,128]{1,2,0:T(8,128)S(1)} custom-call(f32[1,128,128]{2,1,0:T(8,128)S(1)} %get-tuple-element.270), custom_call_target="InvertDiagBlocksLowerTriangular" | custom-call | tf_op jit(solution)/shard_map/jit(cholesky)/cholesky | solution.py:94
  672.8 11.9 %cholesky.233 = f32[128,128]{1,0:T(8,128)S(1)} custom-call(f32[128,128]{1,0:T(8,128)S(1)} %cholesky.273), custom_call_target="Cholesky" | custom-call | tf_op jit(solution)/shard_map/jit(cholesky)/cholesky | solution.py:94
  685.5 9.8 %custom-call.47 = f32[1,128,128]{1,2,0:T(8,128)S(1)} custom-call(f32[1,128,128]{2,1,0:T(8,128)S(1)} %get-tuple-element.267), custom_call_target="InvertDiagBlocksLowerTriangular" | custom-call | tf_op jit(solution)/shard_map/jit(cholesky)/cholesky | solution.py:94
  696.4 4.4 cholesky.253
  704.2 6.1 while.1
  710.4 39.3 %custom-call.48 = f32[4,128,128]{1,2,0:T(8,128)S(1)} custom-call(f32[4,128,128]{2,1,0:T(8,128)S(1)} %pad_maximum_fusion.1), custom_call_target="InvertDiagBlocksLowerTriangular" | custom-call | tf_op jit(solution)/shard_map/jit(_cho_solve)/triangular_solve | solution.py:96
  755.3 26.5 %psum.31 = f32[]{:T(128)} all-reduce(f32[]{:T(128)} %get-tuple-element.278), channel_id=1, replica_groups=mesh['space'=32,'fac'=8] {'fac'}, use_global_device_ids=true, to_apply=%region_16.17 | all-reduce | flops 1 | bytes 8 | tf_op jit(solution)/shard_map/psum | solution.py:98
  (171 shorter events, 91.8 us)
Async XLA Ops:
  8.0 13.9 %copy-start = (bf16[1,2,16,16,128]{4,3,2,1,0:T(8,128)(2,1)S(1)}, bf16[1,2,16,16,128]{4,3,2,1,0:T(8,128)(2,1)}, u32[]{:S(2)}) copy-start(bf16[1,2,16,16,128]{4,3,2,1,0:T(8,128)(2,1)} %param.4) | copy-start | bytes 393220
  8.0 9.5 %copy-start.1 = (bf16[1,2,16,16,128]{4,3,2,1,0:T(8,128)(2,1)S(1)}, bf16[1,2,16,16,128]{4,3,2,1,0:T(8,128)(2,1)}, u32[]{:S(2)}) copy-start(bf16[1,2,16,16,128]{4,3,2,1,0:T(8,128)(2,1)} %param.3) | copy-start | bytes 393220
  8.0 301.4 %all-reduce.8.cloned.1.call-start = ((), (), s32[]{:S(2)}) async-start(), calls=%async_computation.2 | async-start | bytes 131072 | tf_op jit(solution)/shard_map/psum | solution.py:80
  9.9 331.2 %reduce-scatter.5.cloned.1.call-start = ((), (), s32[]{:S(2)}) async-start(), calls=%async_computation.4 | async-start | bytes 1990656 | tf_op jit(solution)/shard_map/reduce_scatter | solution.py:85
  11.0 7.7 collective-permute-start
  15.6 6.3 collective-permute-start.1
  44.4 1.9 copy-start.6
  50.9 4.4 copy-start.11
  89.2 261.8 %reduce-scatter.3.cloned.1.call-start = ((), (), s32[]{:S(2)}) async-start(), calls=%async_computation.3 | async-start | bytes 7962624 | tf_op jit(solution)/shard_map/reduce_scatter | solution.py:84
  92.0 2.7 copy-start.2
  93.3 2.7 copy-start.3
  94.7 2.7 copy-start.4
  96.0 2.7 copy-start.5
  100.1 236.3 %copy-start.10 = (bf16[27,128,128]{2,1,0:T(8,128)(2,1)S(1)}, bf16[27,128,128]{2,1,0:T(8,128)(2,1)}, u32[]{:S(2)}) copy-start(bf16[27,128,128]{2,1,0:T(8,128)(2,1)} %param.5) | copy-start | bytes 2654212
  100.1 521.1 %all-reduce.10.cloned.1.call-start = ((), (), s32[]{:S(2)}) async-start(), calls=%async_computation.5 | async-start | bytes 2211840 | tf_op jit(solution)/shard_map/psum | solution.py:82
  340.3 10.7 %copy-start.12 = (bf16[2,16,16,128]{3,2,1,0:T(8,128)(2,1)S(1)}, bf16[2,16,16,128]{3,2,1,0:T(8,128)(2,1)}, u32[]{:S(2)}) copy-start(bf16[2,16,16,128]{3,2,1,0:T(8,128)(2,1)} %slice.1801) | copy-start | bytes 393220
  622.2 1.7 copy-start.7
  624.1 12.7 %copy-start.8 = (f32[432,432]{1,0:T(8,128)}, f32[432,432]{1,0:T(8,128)S(1)}, u32[]{:S(2)}) copy-start(f32[432,432]{1,0:T(8,128)S(1)} %fusion.25) | copy-start | bytes 2239492
  649.1 55.0 %copy-start.15 = (f32[3,128,128]{2,1,0:T(8,128)S(1)}, f32[3,128,128]{2,1,0:T(8,128)}, u32[]{:S(2)}) copy-start(f32[3,128,128]{2,1,0:T(8,128)} %custom-call.51) | copy-start | bytes 589828
  672.8 37.5 %copy-start.13 = (f32[128,80]{1,0:T(8,128)S(1)}, f32[128,80]{1,0:T(8,128)}, u32[]{:S(2)}) copy-start(f32[128,80]{1,0:T(8,128)} %pad_convert_fusion) | copy-start | bytes 122884
  710.4 43.3 %copy-start.14 = (f32[1,128,128]{1,2,0:T(8,128)S(1)}, f32[1,128,128]{1,2,0:T(8,128)}, u32[]{:S(2)}) copy-start(f32[1,128,128]{1,2,0:T(8,128)} %custom-call.44) | copy-start | bytes 196612
  750.0 4.1 copy-start.9
Sparse Core Ops, SparseCore 0:
  14.4 295.0 all-reduce.7
Sparse Core Ops, SparseCore 1:
  89.3 93.8 reduce-scatter.4
  187.3 163.6 reduce-scatter.2
  353.8 267.4 all-reduce.9
where the time goes:
time: 805 us; the launch traced here: 791 us
  waiting for transfers between devices  490 us (61%)
  other arithmetic  142 us (18%)
  local copies, waits for them, and re-layouts  64.3 us (8%)
  matrix products  41.1 us (5%)
  blocking collectives  26.5 us (3%)
  between operations  20.1 us (2%)
    psum x1, waiting for transfers between devices, on_device(): summed = lax.psum((grams, grads), 'space')  269 us
    psum x1, waiting for transfers between devices, on_device(): cot_total = lax.psum(cot_gram, ('space', 'fac'))  208 us
    another operation x15, other arithmetic, on_device(): left_chol = jnp.linalg.cholesky(left_mat)  72.2 us
    another operation x7, other arithmetic, on_device(): half = jax.scipy.linalg.cho_solve((left_chol, True), scaled)  40.2 us
    concatenate x8, local copies, waits for them, and re-layouts, local_stats(): patch = jnp.concatenate(pieces, axis=1)  30.6 us
    psum x1, blocking collectives, on_device(): total = lax.psum(jnp.sum(raw * scaled), 'fac')  26.5 us
    slice x13, local copies, waits for them, and re-layouts, local_stats(): window(padded_in, shift, extent)[..., lower:lower + width]  25.1 us
  transfers between devices with their start and end apart: 6, of which 4 were waited for; matrix products, arithmetic and copies ran while one was open for 14% of the time, Pallas kernels for 0%

commit v1 on v0

v1 whole, which is shorter than its diff:
```python
import math

import jax
import jax.numpy as jnp
from jax import lax
from jax.experimental import pallas as pl
from jax.experimental.pallas import tpu as pltpu
from jax.sharding import PartitionSpec as P

damping = 0.1
clip_rate = 0.05
TAPS = 27
F32 = jnp.float32
BF16 = jnp.bfloat16
HI = lax.Precision.HIGHEST
VMEM = pl.BlockSpec(memory_space=pltpu.VMEM)
PARAMS = pltpu.CompilerParams(vmem_limit_bytes=48 * 1024 * 1024)

ORDER = 432
EDGES = (0, 128, 256, 384)
STARTS = (0, 432, 736, 912)
GRAD_AT = 960
COT_AT = 1392
PACKED = 1536


def call(body, out_shape, scratch=(), name=None):
    def run(*args):
        return pl.pallas_call(
            body,
            out_shape=out_shape,
            in_specs=[VMEM] * len(args),
            out_specs=jax.tree.map(lambda _: VMEM, out_shape),
            scratch_shapes=list(scratch),
            compiler_params=PARAMS,
            name=name,
        )(*args)

    return run


def nt(a, b, precision=None):
    return lax.dot_general(a, b, (((1,), (1,)), ((), ())), precision=precision, preferred_element_type=F32)


def nn(a, b, precision=None):
    return lax.dot_general(a, b, (((1,), (0,)), ((), ())), precision=precision, preferred_element_type=F32)


def tn(a, b, precision=None):
    return lax.dot_general(a, b, (((0,), (0,)), ((), ())), precision=precision, preferred_element_type=F32)


def prep_kernel(act_ref, cot_ref, send_ref):
    act = act_ref[...].astype(F32).T.astype(BF16)
    cot = cot_ref[...].astype(F32).T.astype(BF16)
    groups = send_ref.shape[0]
    width = act.shape[0] // groups
    for j in range(groups):
        send_ref[j, 0:width, :] = act[j * width : (j + 1) * width]
        send_ref[j, width:, :] = cot


def in_grad_kernel(prev_ref, cot_ref, next_ref, kern_ref, out_ref, rows_ref, shift_ref):
    rows_ref[8:264, :] = prev_ref[...].astype(F32)
    rows_ref[264:776, :] = cot_ref[...].astype(F32)
    rows_ref[776:1032, :] = next_ref[...].astype(F32)
    z = lax.broadcasted_iota(jnp.int32, (256, 128), 0) % 16
    zeros = jnp.zeros((16, 384), BF16)
    for plane in range(4):
        base = plane * 288
        shift_ref[base : base + 16, :] = zeros
        shift_ref[base + 272 : base + 288, :] = zeros
        for n, c in enumerate((-1, 0, 1)):
            at = 8 + plane * 256 + c
            cells = rows_ref[at : at + 256, :]
            if c:
                cells = jnp.where((z + c >= 0) & (z + c < 16), cells, 0.0)
            shift_ref[base + 16 : base + 272, n * 128 : (n + 1) * 128] = cells.astype(BF16)
    for x in range(2):
        total = jnp.zeros((256, 128), F32)
        for a in (-1, 0, 1):
            for b in (-1, 0, 1):
                for n, c in enumerate((-1, 0, 1)):
                    tap = 9 * (1 - a) + 3 * (1 - b) + (1 - c)
                    at = (x + 1 + a) * 288 + 16 + 16 * b
                    rows = shift_ref[at : at + 256, n * 128 : (n + 1) * 128]
                    total = total + nt(rows, kern_ref[tap])
        out_ref[x * 256 : (x + 1) * 256, :] = total.astype(BF16)


def stats_kernel(recv_ref, prev_ref, next_ref, out_ref, x_ref):
    slabs = recv_ref.shape[0]
    lane = lax.broadcasted_iota(jnp.int32, (16, 1024), 1)
    y = (lane // 16) % 16
    z = lane % 16
    for s in range(slabs):
        cols = slice(s * 512, (s + 1) * 512)
        planes = jnp.concatenate([prev_ref[s], recv_ref[s, 0:16, :], next_ref[s]], axis=1).astype(F32)
        for b in (-1, 0, 1):
            for c in (-1, 0, 1):
                d = 16 * b + c
                moved = planes
                if d:
                    moved = pltpu.roll(planes, (-d) % 1024, 1)
                    ok = (y + b >= 0) & (y + b < 16) & (z + c >= 0) & (z + c < 16)
                    moved = jnp.where(ok, moved, 0.0)
                moved = moved.astype(BF16)
                for a in (-1, 0, 1):
                    tap = 9 * (a + 1) + 3 * (b + 1) + (c + 1)
                    at = (1 + a) * 256
                    x_ref[tap * 16 : (tap + 1) * 16, cols] = moved[:, at : at + 512]
        x_ref[ORDER:, cols] = recv_ref[s, 16:, :]
    for edge, start in zip(EDGES, STARTS):
        tile = nt(x_ref[edge:ORDER, :], x_ref[edge : edge + 128, :])
        out_ref[start : start + ORDER - edge, :] = tile
    out_ref[GRAD_AT : GRAD_AT + ORDER + 128, :] = nt(x_ref[...], x_ref[ORDER:, :])
    out_ref[GRAD_AT + ORDER + 128 :, :] = jnp.zeros((PACKED - GRAD_AT - ORDER - 128, 128), F32)


def spread(row):
    return jnp.broadcast_to(row, (8, 128))


def invert(tiles):
    count = len(tiles)
    lane = lax.broadcasted_iota(jnp.int32, (8, 128), 1)
    sub = lax.broadcasted_iota(jnp.int32, (8, 128), 0)
    tiles = list(tiles)
    for g in range(count):
        rows = tiles[g]
        cols = [jnp.broadcast_to(rows[:, 8 * g + q : 8 * g + q + 1], (8, 128)) for q in range(8)]
        for k in range(8):
            pivot = 1.0 / spread(cols[k][k : k + 1, :])
            scaled = cols[k] * pivot
            for q in range(8):
                if q != k:
                    head = spread(cols[q][k : k + 1, :])
                    cols[q] = jnp.where(sub == k, head * pivot, cols[q] - scaled * head)
            cols[k] = jnp.where(sub == k, pivot, -scaled)
        swept = cols[0] * spread(rows[0:1, :])
        for q in range(1, 8):
            swept = swept + cols[q] * spread(rows[q : q + 1, :])
        for q in range(8):
            swept = jnp.where(lane == 8 * g + q, -cols[q], swept)
        heads = [spread(swept[q : q + 1, :]) for q in range(8)]
        inside = (lane >= 8 * g) & (lane < 8 * g + 8)
        for i in range(count):
            if i == g:
                continue
            old = tiles[i]
            new = jnp.where(inside, 0.0, old)
            for q in range(8):
                new = new - jnp.broadcast_to(old[:, 8 * g + q : 8 * g + q + 1], (8, 128)) * heads[q]
            tiles[i] = new
        tiles[g] = swept
    return [-t for t in tiles]


def solve_kernel(stat_ref, raw_ref, part_ref, d_ref, w_ref, t_ref, b_ref, *, count):
    eye = (
        lax.broadcasted_iota(jnp.int32, (128, 128), 0) == lax.broadcasted_iota(jnp.int32, (128, 128), 1)
    ).astype(F32)

    def tile(p):
        edge = EDGES[p]
        rows = stat_ref[STARTS[p] : STARTS[p] + ORDER - edge, :] / count
        if p == 3:
            rows = jnp.where(lax.broadcasted_iota(jnp.int32, rows.shape, 1) < ORDER - edge, rows, 0.0)
        head = min(128, ORDER - edge)
        first = rows[:head] + damping * eye[:head]
        return jnp.concatenate([first, rows[head:]], axis=0) if head < rows.shape[0] else first

    t = [tile(p) for p in range(4)]
    scaled = stat_ref[GRAD_AT : GRAD_AT + ORDER, :] / math.sqrt(count)
    right = stat_ref[COT_AT : COT_AT + 128, :] / count + damping * eye
    for p in range(4):
        t_ref[STARTS[p] : STARTS[p] + ORDER - EDGES[p], :] = t[p]
    b_ref[...] = scaled

    d_ref[0] = right
    d_ref[1] = t[0][:128]
    for p in range(5):
        m = d_ref[p]
        size = 128 if p < 4 else ORDER - EDGES[3]
        inv = invert([m[8 * i : 8 * i + 8] for i in range(size // 8)])
        for i in range(size // 8):
            w_ref[p, 8 * i : 8 * i + 8, :] = inv[i]
        if 1 <= p < 4:
            q = p - 1
            edge = EDGES[q]
            below = t_ref[STARTS[q] + 128 : STARTS[q] + ORDER - edge, :]
            y = nn(below, w_ref[p], HI)
            t_ref[STARTS[q] + 128 : STARTS[q] + ORDER - edge, :] = y
            b_ref[edge + 128 :, :] = b_ref[edge + 128 :, :] - nn(y, b_ref[edge : edge + 128, :], HI)
            for r in range(q + 1, 4):
                lo = EDGES[r] - EDGES[q] - 128
                head = min(128, ORDER - EDGES[r])
                part = below[lo : lo + head]
                if head < 128:
                    part = jnp.concatenate([part, jnp.zeros((128 - head, 128), F32)], axis=0)
                span = slice(STARTS[r], STARTS[r] + ORDER - EDGES[r])
                new = t_ref[span, :] - nt(y[lo:], part, HI)
                t_ref[span, :] = new
                if r == q + 1:
                    d_ref[p + 1, 0:head, :] = new[:head]
    x3 = nn(w_ref[4, 0:48, 0:48], b_ref[384:432, :], HI)
    raw_ref[384:432, :] = x3
    for q in (2, 1, 0):
        edge = EDGES[q]
        y = t_ref[STARTS[q] + 128 : STARTS[q] + ORDER - edge, :]
        x = nn(w_ref[q + 1], b_ref[edge : edge + 128, :], HI) - tn(y, raw_ref[edge + 128 :, :], HI)
        raw_ref[edge : edge + 128, :] = x
    raw = nn(raw_ref[...], w_ref[0], HI)
    raw_ref[...] = raw
    prod = raw * (stat_ref[GRAD_AT : GRAD_AT + ORDER, :] / math.sqrt(count))
    acc = prod[0:8]
    for i in range(1, ORDER // 8):
        acc = acc + prod[8 * i : 8 * i + 8]
    part_ref[...] = jnp.broadcast_to(jnp.sum(acc).reshape(1, 1), (8, 128))


def on_device(activations, out_grad, kernel):
    shape = activations.shape
    spaces = lax.axis_size("space")
    groups = lax.axis_size("fac")
    act = activations.reshape(512, 128)
    cot = out_grad.reshape(512, 128)
    up = [(i, i + 1) for i in range(spaces - 1)]
    down = [(i + 1, i) for i in range(spaces - 1)]

    cot_prev = lax.ppermute(cot[256:], "space", up)
    cot_next = lax.ppermute(cot[:256], "space", down)

    send = call(prep_kernel, jax.ShapeDtypeStruct((groups, 144, 512), BF16), name="prep")(act, cot)
    recv = lax.all_to_all(send, "fac", 0, 0, tiled=True)
    act_prev = lax.ppermute(recv[:, :16, 256:], "space", up)
    act_next = lax.ppermute(recv[:, :16, :256], "space", down)

    in_grad = call(
        in_grad_kernel,
        jax.ShapeDtypeStruct((512, 128), BF16),
        scratch=[pltpu.VMEM((1040, 128), F32), pltpu.VMEM((1152, 384), BF16)],
        name="in_grad",
    )(cot_prev, cot, cot_next, kernel)

    stats = call(
        stats_kernel,
        jax.ShapeDtypeStruct((PACKED, 128), F32),
        scratch=[pltpu.VMEM((ORDER + 128, groups * 512), BF16)],
        name="stats",
    )(recv, act_prev, act_next)

    share = PACKED // spaces
    parts = lax.all_to_all(stats.reshape(spaces, share, 128), "space", 0, 0, tiled=True)
    mine = jnp.sum(parts, axis=0)
    whole = lax.all_to_all(jnp.broadcast_to(mine[None], (spaces, share, 128)), "space", 0, 0, tiled=True)

    count = float(512 * spaces * groups)

    def body(*refs):
        solve_kernel(*refs, count=count)

    raw, part = call(
        body,
        (jax.ShapeDtypeStruct((ORDER, 128), F32), jax.ShapeDtypeStruct((8, 128), F32)),
        scratch=[
            pltpu.VMEM((5, 128, 128), F32),
            pltpu.VMEM((5, 128, 128), F32),
            pltpu.VMEM((960, 128), F32),
            pltpu.VMEM((ORDER, 128), F32),
        ],
        name="solve",
    )(whole.reshape(PACKED, 128))
    total = part
    for bit in (1, 2, 4):
        total = total + lax.ppermute(total, "fac", [(i, i ^ bit) for i in range(groups)])
    factor = jnp.sqrt(clip_rate * kernel.size / total[0, 0])
    update = raw.reshape(TAPS, 16, 128) * factor
    return (in_grad.reshape(shape), update)


def solution(mesh):
    placed = (P("fac", "space", None, None, None), P("fac", "space", None, None, None), P())
    return jax.shard_map(
        on_device,
        mesh=mesh,
        in_specs=placed,
        out_specs=(P("fac", "space", None, None, None), P(None, "fac", None)),
        check_vma=False,
    )
```

time: 805 us -> 153 us (0.19); the launches traced: 791 us -> 152 us
  waiting for transfers between devices: 490 us -> 29.4 us
  other arithmetic: 142 us -> 0.77 us
  local copies, waits for them, and re-layouts: 64.3 us -> 3.3 us
  matrix products: 41.1 us -> 0 us
  blocking collectives: 26.5 us -> 63.9 us
  Pallas kernels: 0 us -> 26.6 us
  starting transfers between devices: 6.86 us -> 26.3 us
  between operations: 20.1 us -> 1.48 us
    psum x2 -> x0, waiting for transfers between devices: 477 us -> none  [the longest x1 269 us: on_device(): summed = lax.psum((grams, grads), 'space')]
    another operation x27 -> x0, other arithmetic: 136 us -> none  [the longest x15 72.2 us: on_device(): left_chol = jnp.linalg.cholesky(left_mat)]
    all_to_all x0 -> x2, blocking collectives: none -> 63.9 us  [the longest x1 33.4 us: on_device(): recv = lax.all_to_all(send, 'fac', 0, 0, tiled=True)]
    dot_general x44 -> x0, matrix products: 30.7 us -> none  [the longest x8 12.3 us: local_stats(): jnp.dot(patch.T, rows_cot, preferred_element_type=jnp.float32)]
    concatenate x8 -> x0, local copies, waits for them, and re-layouts: 30.6 us -> none  [local_stats(): patch = jnp.concatenate(pieces, axis=1)]
    pallas_call x0 -> x4, Pallas kernels: none -> 26.6 us  [run(): pl.pallas_call(body, out_shape=out_shape, in_specs=[VMEM] * len(args), ou...]
    slice x17 -> x3, local copies, waits for them, and re-layouts: 27.1 us -> 0.54 us  [the longest x1 0.51 us: on_device(): factor = jnp.sqrt(clip_rate * kernel.size / total[0, 0])]
    psum x1 -> x0, blocking collectives: 26.5 us -> none  [on_device(): total = lax.psum(jnp.sum(raw * scaled), 'fac')]
  transfers between devices with their start and end apart: 6 -> 8, of which waited for: 4 -> 5; matrix products, arithmetic and copies ran while one was open for 14% -> 0% of each run, Pallas kernels for 0% -> 15%
where the time goes in v1:
time: 153 us; the launch traced here: 152 us
  blocking collectives  63.9 us (42%)
  waiting for transfers between devices  29.4 us (19%)
  Pallas kernels  26.6 us (17%)
  starting transfers between devices  26.3 us (17%)
  local copies, waits for them, and re-layouts  3.3 us (2%)
    all_to_all x1, blocking collectives, on_device(): recv = lax.all_to_all(send, 'fac', 0, 0, tiled=True)  33.4 us
    all_to_all x1, blocking collectives, on_device(): lax.all_to_all(stats.reshape(spaces, share, 128), 'space', 0, 0, tiled=True)  30.5 us
    pallas_call x4, Pallas kernels, run(): pl.pallas_call(body, out_shape=out_shape, in_specs=[VMEM] * len(args), ou...  26.6 us
    all_to_all x1, waiting for transfers between devices, on_device(): lax.all_to_all(jnp.broadcast_to(mine[None], (spaces, share, 128)), 'space...  15.9 us
    ppermute x1, starting transfers between devices, on_device(): act_prev = lax.ppermute(recv[:, :16, 256:], 'space', up)  12.6 us
    ppermute x3, waiting for transfers between devices, on_device(): lax.ppermute(total, 'fac', [(i, i ^ bit) for i in range(groups)])  9.85 us
    all_to_all x1, starting transfers between devices, on_device(): lax.all_to_all(jnp.broadcast_to(mine[None], (spaces, share, 128)), 'space...  4.76 us
    ppermute x1, waiting for transfers between devices, on_device(): act_next = lax.ppermute(recv[:, :16, :256], 'space', down)  3.65 us
  transfers between devices with their start and end apart: 8, of which 5 were waited for; matrix products, arithmetic and copies ran while one was open for 0% of the time, Pallas kernels for 15%

profile of v1, /device:TPU:1, one launch (start us, length us, event | category | flops | bytes accessed | tf_op | source)
XLA Modules:
  0.0 151.7 jit_solution(4178656314507717082)
XLA Ops:
  0.6 0.9 copy-done
  1.5 0.9 copy-done.3
  2.4 0.2 prep.1
  2.6 33.4 %all_to_all.15.recv_ref = bf16[8,144,512]{2,1,0:T(8,128)(2,1)S(1)} all-to-all(bf16[8,144,512]{2,1,0:T(8,128)(2,1)S(1)} %prep.1), channel_id=1, replica_groups=mesh['space'=32,'fac'=8] {'fac'}, dimensions={0} | all-to-all | bytes 2359296 | tf_op jit(solution)/shard_map/all_to_all | solution.py:236
  36.0 12.6 %collective-permute-start.2 = (bf16[8,16,256]{2,1,0:T(8,128)(2,1)S(1)}, bf16[8,16,256]{2,1,0:T(8,128)(2,1)S(1)}, u32[]{:S(2)}, u32[]{:S(2)}) collective-permute-start(bf16[8,16,256]{2,1,0:T(8,128)(2,1)S(1)} %get-tuple-element.7), channel_id=1, source_target_pairs={{0,8},{8,16},{16,24},{24,32},{32,40},{40,48},{48,56},{56,64},{64,7... | collective-permute-start | bytes 196616 | tf_op jit(solution)/shard_map/ppermute | solution.py:237
  48.6 1.9 %collective-permute-start.3 = (bf16[8,16,256]{2,1,0:T(8,128)(2,1)S(1)}, bf16[8,16,256]{2,1,0:T(8,128)(2,1)S(1)}, u32[]{:S(2)}, u32[]{:S(2)}) collective-permute-start(bf16[8,16,256]{2,1,0:T(8,128)(2,1)S(1)} %get-tuple-element.6), channel_id=1, source_target_pairs={{8,0},{16,8},{24,16},{32,24},{40,32},{48,40},{56,48},{64,56},{72,6... | collective-permute-start | bytes 196616 | tf_op jit(solution)/shard_map/ppermute | solution.py:238
  50.6 3.6 %collective-permute-done.3.next_ref = bf16[8,16,256]{2,1,0:T(8,128)(2,1)S(1)} collective-permute-done((bf16[8,16,256]{2,1,0:T(8,128)(2,1)S(1)}, bf16[8,16,256]{2,1,0:T(8,128)(2,1)S(1)}, u32[]{:S(2)}, u32[]{:S(2)}) %collective-permute-start.3) | collective-permute-done | bytes 65568 | tf_op jit(solution)/shard_map/ppermute | solution.py:238
  54.2 3.6 %stats.1 = f32[1536,128]{1,0:T(8,128)S(1)} custom-call(bf16[8,144,512]{2,1,0:T(8,128)(2,1)S(1)} %all_to_all.15.recv_ref, bf16[8,16,256]{2,1,0:T(8,128)(2,1)S(1)} %collective-permute-done.2.prev_ref, bf16[8,16,256]{2,1,0:T(8,128)(2,1)S(1)} %collective-permute-done.3.next_ref), custom_call_target="tpu_custom_call" | custom-call | tf_op jit(solution)/shard_map/stats/pallas_call | solution.py:29
  57.9 30.5 %all_to_all.16 = f32[32,48,128]{2,1,0:T(8,128)S(1)} all-to-all(f32[32,48,128]{2,1,0:T(8,128)S(1)} %bitcast.10), channel_id=1, replica_groups=mesh['space'=32,'fac'=8] {'space'}, dimensions={0} | all-to-all | bytes 1572864 | tf_op jit(solution)/shard_map/all_to_all | solution.py:255
  88.5 0.9 broadcast_in_dim.2
  89.4 4.8 %all-to-all-start.2 = ((f32[32,48,128]{2,1,0:T(8,128)}), f32[32,48,128]{2,1,0:T(8,128)S(1)}, u32[]{:S(2)}, u32[]{:S(2)}) async-start(f32[32,48,128]{2,1,0:T(8,128)} %broadcast_in_dim.2), calls=%async_computation.2 | async-start | bytes 1572864 | tf_op jit(solution)/shard_map/all_to_all | solution.py:257
  94.2 3.5 %collective-permute-start = (bf16[256,128]{1,0:T(8,128)(2,1)S(1)}, bf16[256,128]{1,0:T(8,128)(2,1)S(1)}, u32[]{:S(2)}, u32[]{:S(2)}) collective-permute-start(bf16[256,128]{1,0:T(8,128)(2,1)S(1)} %bitcast.17), channel_id=1, source_target_pairs={{0,8},{8,16},{16,24},{24,32},{32,40},{40,48},{48,56},{56,64},{64,7... | collective-permute-start | bytes 196616 | tf_op jit(solution)/shard_map/ppermute | solution.py:232
  97.8 2.1 %collective-permute-start.1 = (bf16[256,128]{1,0:T(8,128)(2,1)S(1)}, bf16[256,128]{1,0:T(8,128)(2,1)S(1)}, u32[]{:S(2)}, u32[]{:S(2)}) collective-permute-start(bf16[256,128]{1,0:T(8,128)(2,1)S(1)} %bitcast.16), channel_id=1, source_target_pairs={{8,0},{16,8},{24,16},{32,24},{40,32},{48,40},{56,48},{64,56},{72,6... | collective-permute-start | bytes 196616 | tf_op jit(solution)/shard_map/ppermute | solution.py:233
  99.9 15.9 %all-to-all-done.2 = f32[32,48,128]{2,1,0:T(8,128)S(1)} async-done(((f32[32,48,128]{2,1,0:T(8,128)}), f32[32,48,128]{2,1,0:T(8,128)S(1)}, u32[]{:S(2)}, u32[]{:S(2)}) %all-to-all-start.2) | async-done | bytes 786464 | tf_op jit(solution)/shard_map/all_to_all | solution.py:257
  115.7 21.0 %solve.1 = (f32[432,128]{1,0:T(8,128)S(1)}, f32[8,128]{1,0:T(8,128)S(1)}) custom-call(f32[1536,128]{1,0:T(8,128)S(1)} %bitcast.9), custom_call_target="tpu_custom_call" | custom-call | tf_op jit(solution)/shard_map/solve/pallas_call | solution.py:29
  136.8 0.3 collective-permute-start.4
  137.1 2.3 %collective-permute-done.4 = f32[8,128]{1,0:T(8,128)S(1)} collective-permute-done((f32[8,128]{1,0:T(8,128)S(1)}, f32[8,128]{1,0:T(8,128)S(1)}, u32[]{:S(2)}, u32[]{:S(2)}) %collective-permute-start.4) | collective-permute-done | bytes 4128 | tf_op jit(solution)/shard_map/ppermute | solution.py:277
  139.4 0.7 collective-permute-start.5
  140.1 3.3 %collective-permute-done.5 = f32[8,128]{1,0:T(8,128)S(1)} collective-permute-done((f32[8,128]{1,0:T(8,128)S(1)}, f32[8,128]{1,0:T(8,128)S(1)}, u32[]{:S(2)}, u32[]{:S(2)}) %collective-permute-start.5) | collective-permute-done | bytes 4128 | tf_op jit(solution)/shard_map/ppermute | solution.py:277
  143.4 0.4 collective-permute-start.6
  143.8 1.8 %in_grad.1 = bf16[512,128]{1,0:T(8,128)(2,1)} custom-call(bf16[256,128]{1,0:T(8,128)(2,1)S(1)} %collective-permute-done.prev_ref, bf16[512,128]{1,0:T(8,128)(2,1)S(1)} %bitcast.12, bf16[256,128]{1,0:T(8,128)(2,1)S(1)} %collective-permute-done.1.next_ref, bf16[27,128,128]{2,1,0:T(8,128)(2,1)S(1)} %copy-done.2), custom_call_target="tpu_custom_call" | custom-call | tf_op jit(solution)/shard_map/in_grad/pallas_call | solution.py:29
  145.5 4.2 %collective-permute-done.6 = f32[8,128]{1,0:T(8,128)S(1)} collective-permute-done((f32[8,128]{1,0:T(8,128)S(1)}, f32[8,128]{1,0:T(8,128)S(1)}, u32[]{:S(2)}, u32[]{:S(2)}) %collective-permute-start.6) | collective-permute-done | bytes 4128 | tf_op jit(solution)/shard_map/ppermute | solution.py:277
  149.7 0.5 slice.27
  151.0 0.7 broadcast_multiply_fusion
  (15 shorter events, 0.1 us)
Async XLA Ops:
  0.6 0.9 copy-start
  1.5 0.9 copy-start.3
  36.0 14.6 %collective-permute-start.2 = (bf16[8,16,256]{2,1,0:T(8,128)(2,1)S(1)}, bf16[8,16,256]{2,1,0:T(8,128)(2,1)S(1)}, u32[]{:S(2)}, u32[]{:S(2)}) collective-permute-start(bf16[8,16,256]{2,1,0:T(8,128)(2,1)S(1)} %get-tuple-element.7), channel_id=1, source_target_pairs={{0,8},{8,16},{16,24},{24,32},{32,40},{40,48},{48,56},{56,64},{64,7... | collective-permute-start | bytes 196616 | tf_op jit(solution)/shard_map/ppermute | solution.py:237
  48.6 5.6 %collective-permute-start.3 = (bf16[8,16,256]{2,1,0:T(8,128)(2,1)S(1)}, bf16[8,16,256]{2,1,0:T(8,128)(2,1)S(1)}, u32[]{:S(2)}, u32[]{:S(2)}) collective-permute-start(bf16[8,16,256]{2,1,0:T(8,128)(2,1)S(1)} %get-tuple-element.6), channel_id=1, source_target_pairs={{8,0},{16,8},{24,16},{32,24},{40,32},{48,40},{56,48},{64,56},{72,6... | collective-permute-start | bytes 196616 | tf_op jit(solution)/shard_map/ppermute | solution.py:238
  88.5 5.7 %copy-start.1 = (bf16[1,2,16,16,128]{4,3,2,1,0:T(8,128)(2,1)S(1)}, bf16[1,2,16,16,128]{4,3,2,1,0:T(8,128)(2,1)}, u32[]{:S(2)}) copy-start(bf16[1,2,16,16,128]{4,3,2,1,0:T(8,128)(2,1)} %param.4) | copy-start | bytes 393220
  89.4 54.3 %copy-start.2 = (bf16[27,128,128]{2,1,0:T(8,128)(2,1)S(1)}, bf16[27,128,128]{2,1,0:T(8,128)(2,1)}, u32[]{:S(2)}) copy-start(bf16[27,128,128]{2,1,0:T(8,128)(2,1)} %kern_ref.1) | copy-start | bytes 2654212
  89.4 26.3 %all-to-all-start.2 = ((f32[32,48,128]{2,1,0:T(8,128)}), f32[32,48,128]{2,1,0:T(8,128)S(1)}, u32[]{:S(2)}, u32[]{:S(2)}) async-start(f32[32,48,128]{2,1,0:T(8,128)} %broadcast_in_dim.2), calls=%async_computation.2 | async-start | bytes 1572864 | tf_op jit(solution)/shard_map/all_to_all | solution.py:257
  94.2 49.5 %collective-permute-start = (bf16[256,128]{1,0:T(8,128)(2,1)S(1)}, bf16[256,128]{1,0:T(8,128)(2,1)S(1)}, u32[]{:S(2)}, u32[]{:S(2)}) collective-permute-start(bf16[256,128]{1,0:T(8,128)(2,1)S(1)} %bitcast.17), channel_id=1, source_target_pairs={{0,8},{8,16},{16,24},{24,32},{32,40},{40,48},{48,56},{56,64},{64,7... | collective-permute-start | bytes 196616 | tf_op jit(solution)/shard_map/ppermute | solution.py:232
  97.8 46.0 %collective-permute-start.1 = (bf16[256,128]{1,0:T(8,128)(2,1)S(1)}, bf16[256,128]{1,0:T(8,128)(2,1)S(1)}, u32[]{:S(2)}, u32[]{:S(2)}) collective-permute-start(bf16[256,128]{1,0:T(8,128)(2,1)S(1)} %bitcast.16), channel_id=1, source_target_pairs={{8,0},{16,8},{24,16},{32,24},{40,32},{48,40},{56,48},{64,56},{72,6... | collective-permute-start | bytes 196616 | tf_op jit(solution)/shard_map/ppermute | solution.py:233
  136.8 2.6 %collective-permute-start.4 = (f32[8,128]{1,0:T(8,128)S(1)}, f32[8,128]{1,0:T(8,128)S(1)}, u32[]{:S(2)}, u32[]{:S(2)}) collective-permute-start(f32[8,128]{1,0:T(8,128)S(1)} %get-tuple-element.5), channel_id=1, source_target_pairs={{0,1},{1,0},{2,3},{3,2},{4,5},{5,4},{6,7},{7,6},{8,9},{9,8},{10,11... | collective-permute-start | bytes 12296 | tf_op jit(solution)/shard_map/ppermute | solution.py:277
  139.4 4.0 %collective-permute-start.5 = (f32[8,128]{1,0:T(8,128)S(1)}, f32[8,128]{1,0:T(8,128)S(1)}, u32[]{:S(2)}, u32[]{:S(2)}) collective-permute-start(f32[8,128]{1,0:T(8,128)S(1)} %add.9), channel_id=1, source_target_pairs={{0,2},{1,3},{2,0},{3,1},{4,6},{5,7},{6,4},{7,5},{8,10},{9,11},{10,... | collective-permute-start | bytes 12296 | tf_op jit(solution)/shard_map/ppermute | solution.py:277
  143.4 6.4 %collective-permute-start.6 = (f32[8,128]{1,0:T(8,128)S(1)}, f32[8,128]{1,0:T(8,128)S(1)}, u32[]{:S(2)}, u32[]{:S(2)}) collective-permute-start(f32[8,128]{1,0:T(8,128)S(1)} %add.10), channel_id=1, source_target_pairs={{0,4},{1,5},{2,6},{3,7},{4,0},{5,1},{6,2},{7,3},{8,12},{9,13},{10,... | collective-permute-start | bytes 12296 | tf_op jit(solution)/shard_map/ppermute | solution.py:277

commit v2 on v1

--- a/solution.py
+++ b/solution.py
@@ -1,3 +1,4 @@
+import functools
 import math
 
 import jax
@@ -22,6 +23,10 @@
 GRAD_AT = 960
 COT_AT = 1392
 PACKED = 1536
+HALF = PACKED // 2
+
+
+SMEM = pl.BlockSpec(memory_space=pltpu.SMEM)
 
 
 def call(body, out_shape, scratch=(), name=None):
@@ -29,7 +34,7 @@
         return pl.pallas_call(
             body,
             out_shape=out_shape,
-            in_specs=[VMEM] * len(args),
+            in_specs=[SMEM if a.dtype == jnp.int32 else VMEM for a in args],
             out_specs=jax.tree.map(lambda _: VMEM, out_shape),
             scratch_shapes=list(scratch),
             compiler_params=PARAMS,
@@ -51,14 +56,23 @@
     return lax.dot_general(a, b, (((0,), (0,)), ((), ())), precision=precision, preferred_element_type=F32)
 
 
-def prep_kernel(act_ref, cot_ref, send_ref):
-    act = act_ref[...].astype(F32).T.astype(BF16)
+def prep_kernel(high_ref, act_ref, cot_ref, keep_ref, give_ref, act_t):
+    half = act_ref.shape[1] // 2
+    act_t[...] = act_ref[...].astype(F32).T.astype(BF16)
     cot = cot_ref[...].astype(F32).T.astype(BF16)
-    groups = send_ref.shape[0]
-    width = act.shape[0] // groups
-    for j in range(groups):
-        send_ref[j, 0:width, :] = act[j * width : (j + 1) * width]
-        send_ref[j, width:, :] = cot
+    high = high_ref[0]
+    keep_ref[0:half, :] = act_t[pl.ds(pl.multiple_of(high * half, half), half), :]
+    give_ref[0:half, :] = act_t[pl.ds(pl.multiple_of((1 - high) * half, half), half), :]
+    keep_ref[half:, :] = cot
+    give_ref[half:, :] = cot
+
+
+def spread_kernel(keep_ref, got_ref, send_ref):
+    peers = send_ref.shape[0]
+    for n, ref in enumerate((keep_ref, got_ref)):
+        for p in range(peers):
+            send_ref[p, n, 0:16, :] = ref[16 * p : 16 * p + 16, :]
+            send_ref[p, n, 16:, :] = ref[16 * peers :, :]
 
 
 def in_grad_kernel(prev_ref, cot_ref, next_ref, kern_ref, out_ref, rows_ref, shift_ref):
@@ -89,7 +103,17 @@
         out_ref[x * 256 : (x + 1) * 256, :] = total.astype(BF16)
 
 
-def stats_kernel(recv_ref, prev_ref, next_ref, out_ref, x_ref):
+def stats_kernel(core_ref, recv_ref, prev_ref, next_ref, out_ref, x_ref):
+    core = core_ref[0]
+    slots = (core, 1 - core)
+
+    def store(start, value):
+        stop = start + value.shape[0]
+        for h in range(2):
+            lo, hi = max(start, h * HALF), min(stop, (h + 1) * HALF)
+            if lo < hi:
+                out_ref[slots[h], lo - h * HALF : hi - h * HALF, :] = value[lo - start : hi - start]
+
     slabs = recv_ref.shape[0]
     lane = lax.broadcasted_iota(jnp.int32, (16, 1024), 1)
     y = (lane // 16) % 16
@@ -113,51 +137,75 @@
         x_ref[ORDER:, cols] = recv_ref[s, 16:, :]
     for edge, start in zip(EDGES, STARTS):
         tile = nt(x_ref[edge:ORDER, :], x_ref[edge : edge + 128, :])
-        out_ref[start : start + ORDER - edge, :] = tile
-    out_ref[GRAD_AT : GRAD_AT + ORDER + 128, :] = nt(x_ref[...], x_ref[ORDER:, :])
-    out_ref[GRAD_AT + ORDER + 128 :, :] = jnp.zeros((PACKED - GRAD_AT - ORDER - 128, 128), F32)
+        store(start, tile)
+    store(GRAD_AT, nt(x_ref[...], x_ref[ORDER:, :]))
+    store(COT_AT + 128, jnp.zeros((PACKED - COT_AT - 128, 128), F32))
+
+
+def fold_kernel(parts_ref, out_ref):
+    peers = parts_ref.shape[0]
+    total = parts_ref[0]
+    for p in range(1, peers):
+        total = total + parts_ref[p]
+    for p in range(peers):
+        out_ref[p] = total
+
+
+def scale_kernel(raw_ref, parts_ref, out_ref, *, size):
+    total = parts_ref[0]
+    for p in range(1, parts_ref.shape[0]):
+        total = total + parts_ref[p]
+    factor = jnp.sqrt(clip_rate * size / total)[0:1, :]
+    out_ref[...] = raw_ref[...] * factor
 
 
 def spread(row):
     return jnp.broadcast_to(row, (8, 128))
 
 
-def invert(tiles):
-    count = len(tiles)
+def sweep(tiles, g):
     lane = lax.broadcasted_iota(jnp.int32, (8, 128), 1)
     sub = lax.broadcasted_iota(jnp.int32, (8, 128), 0)
-    tiles = list(tiles)
-    for g in range(count):
-        rows = tiles[g]
-        cols = [jnp.broadcast_to(rows[:, 8 * g + q : 8 * g + q + 1], (8, 128)) for q in range(8)]
-        for k in range(8):
-            pivot = 1.0 / spread(cols[k][k : k + 1, :])
-            scaled = cols[k] * pivot
-            for q in range(8):
-                if q != k:
-                    head = spread(cols[q][k : k + 1, :])
-                    cols[q] = jnp.where(sub == k, head * pivot, cols[q] - scaled * head)
-            cols[k] = jnp.where(sub == k, pivot, -scaled)
-        swept = cols[0] * spread(rows[0:1, :])
-        for q in range(1, 8):
-            swept = swept + cols[q] * spread(rows[q : q + 1, :])
+    rows = tiles[g]
+    cols = [jnp.broadcast_to(rows[:, 8 * g + q : 8 * g + q + 1], (8, 128)) for q in range(8)]
+    for k in range(8):
+        pivot = 1.0 / spread(cols[k][k : k + 1, :])
+        scaled = cols[k] * pivot
         for q in range(8):
-            swept = jnp.where(lane == 8 * g + q, -cols[q], swept)
-        heads = [spread(swept[q : q + 1, :]) for q in range(8)]
-        inside = (lane >= 8 * g) & (lane < 8 * g + 8)
-        for i in range(count):
-            if i == g:
-                continue
-            old = tiles[i]
-            new = jnp.where(inside, 0.0, old)
-            for q in range(8):
-                new = new - jnp.broadcast_to(old[:, 8 * g + q : 8 * g + q + 1], (8, 128)) * heads[q]
-            tiles[i] = new
-        tiles[g] = swept
-    return [-t for t in tiles]
-
-
-def solve_kernel(stat_ref, raw_ref, part_ref, d_ref, w_ref, t_ref, b_ref, *, count):
+            if q != k:
+                head = spread(cols[q][k : k + 1, :])
+                cols[q] = jnp.where(sub == k, head * pivot, cols[q] - scaled * head)
+        cols[k] = jnp.where(sub == k, pivot, -scaled)
+    swept = cols[0] * spread(rows[0:1, :])
+    for q in range(1, 8):
+        swept = swept + cols[q] * spread(rows[q : q + 1, :])
+    for q in range(8):
+        swept = jnp.where(lane == 8 * g + q, -cols[q], swept)
+    heads = [spread(swept[q : q + 1, :]) for q in range(8)]
+    inside = (lane >= 8 * g) & (lane < 8 * g + 8)
+    out = []
+    for i, old in enumerate(tiles):
+        if i == g:
+            out.append(swept)
+            continue
+        new = jnp.where(inside, 0.0, old)
+        for q in range(8):
+            new = new - jnp.broadcast_to(old[:, 8 * g + q : 8 * g + q + 1], (8, 128)) * heads[q]
+        out.append(new)
+    return out
+
+
+def invert(*mats):
+    held = [[m[8 * i : 8 * i + 8] for i in range(m.shape[0] // 8)] for m in mats]
+    for g in range(len(held[0])):
+        held = [sweep(tiles, g) for tiles in held]
+    return [[-t for t in tiles] for tiles in held]
+
+
+def solve_kernel(core_ref, mine_ref, other_ref, raw_ref, part_ref, stat_ref, d_ref, w_ref, t_ref, b_ref, *, count):
+    core = core_ref[0]
+    stat_ref[pl.ds(pl.multiple_of(core * HALF, HALF), HALF), :] = mine_ref[...]
+    stat_ref[pl.ds(pl.multiple_of((1 - core) * HALF, HALF), HALF), :] = other_ref[...]
     eye = (
         lax.broadcasted_iota(jnp.int32, (128, 128), 0) == lax.broadcasted_iota(jnp.int32, (128, 128), 1)
     ).astype(F32)
@@ -180,13 +228,13 @@
 
     d_ref[0] = right
     d_ref[1] = t[0][:128]
-    for p in range(5):
-        m = d_ref[p]
+    for p in range(1, 5):
         size = 128 if p < 4 else ORDER - EDGES[3]
-        inv = invert([m[8 * i : 8 * i + 8] for i in range(size // 8)])
-        for i in range(size // 8):
-            w_ref[p, 8 * i : 8 * i + 8, :] = inv[i]
-        if 1 <= p < 4:
+        at = (0, 1) if p == 1 else (p,)
+        for n, inv in zip(at, invert(*[d_ref[n, 0:size, :] for n in at])):
+            for i in range(size // 8):
+                w_ref[n, 8 * i : 8 * i + 8, :] = inv[i]
+        if p < 4:
             q = p - 1
             edge = EDGES[q]
             below = t_ref[STARTS[q] + 128 : STARTS[q] + ORDER - edge, :]
@@ -217,7 +265,7 @@
     acc = prod[0:8]
     for i in range(1, ORDER // 8):
         acc = acc + prod[8 * i : 8 * i + 8]
-    part_ref[...] = jnp.broadcast_to(jnp.sum(acc).reshape(1, 1), (8, 128))
+    part_ref[...] = jnp.broadcast_to(jnp.sum(acc).reshape(1, 1, 1), part_ref.shape)
 
 
 def on_device(activations, out_grad, kernel):
@@ -232,8 +280,19 @@
     cot_prev = lax.ppermute(cot[256:], "space", up)
     cot_next = lax.ppermute(cot[:256], "space", down)
 
-    send = call(prep_kernel, jax.ShapeDtypeStruct((groups, 144, 512), BF16), name="prep")(act, cot)
-    recv = lax.all_to_all(send, "fac", 0, 0, tiled=True)
+    wide = groups // 2
+    high = (lax.axis_index("fac") // wide).astype(jnp.int32).reshape(1)
+    core = (lax.axis_index("space") % 2).astype(jnp.int32).reshape(1)
+    keep, give = call(
+        prep_kernel,
+        (jax.ShapeDtypeStruct((192, 512), BF16),) * 2,
+        scratch=[pltpu.VMEM((128, 512), BF16)],
+        name="prep",
+    )(high, act, cot)
+    got = lax.ppermute(give, "fac", [(i, (i + wide) % groups) for i in range(groups)])
+    send = call(spread_kernel, jax.ShapeDtypeStruct((wide, 2, 144, 512), BF16), name="spread")(keep, got)
+    along_x = [[h * wide + x for x in range(wide)] for h in range(2)]
+    recv = lax.all_to_all(send, "fac", 0, 0, axis_index_groups=along_x, tiled=True).reshape(groups, 144, 512)
     act_prev = lax.ppermute(recv[:, :16, 256:], "space", up)
     act_next = lax.ppermute(recv[:, :16, :256], "space", down)
 
@@ -246,38 +305,42 @@
 
     stats = call(
         stats_kernel,
-        jax.ShapeDtypeStruct((PACKED, 128), F32),
+        jax.ShapeDtypeStruct((2, HALF, 128), F32),
         scratch=[pltpu.VMEM((ORDER + 128, groups * 512), BF16)],
         name="stats",
-    )(recv, act_prev, act_next)
-
-    share = PACKED // spaces
-    parts = lax.all_to_all(stats.reshape(spaces, share, 128), "space", 0, 0, tiled=True)
-    mine = jnp.sum(parts, axis=0)
-    whole = lax.all_to_all(jnp.broadcast_to(mine[None], (spaces, share, 128)), "space", 0, 0, tiled=True)
-
-    count = float(512 * spaces * groups)
-
-    def body(*refs):
-        solve_kernel(*refs, count=count)
+    )(core, recv, act_prev, act_next)
+
+    swap = [(i, i ^ 1) for i in range(spaces)]
+    chips = spaces // 2
+    share = HALF // chips
+    plane = [[2 * i + c for i in range(chips)] for c in range(2)]
+    both = stats[0] + lax.ppermute(stats[1], "space", swap)
+    parts = lax.all_to_all(
+        both.reshape(chips, share, 128), "space", 0, 0, axis_index_groups=plane, tiled=True
+    )
+    copies = call(fold_kernel, jax.ShapeDtypeStruct((chips, share, 128), F32), name="fold")(parts)
+    mine = lax.all_to_all(copies, "space", 0, 0, axis_index_groups=plane, tiled=True).reshape(HALF, 128)
+    other = lax.ppermute(mine, "space", swap)
 
     raw, part = call(
-        body,
-        (jax.ShapeDtypeStruct((ORDER, 128), F32), jax.ShapeDtypeStruct((8, 128), F32)),
+        functools.partial(solve_kernel, count=float(512 * spaces * groups)),
+        (jax.ShapeDtypeStruct((ORDER, 128), F32), jax.ShapeDtypeStruct((groups, 8, 128), F32)),
         scratch=[
+            pltpu.VMEM((PACKED, 128), F32),
             pltpu.VMEM((5, 128, 128), F32),
             pltpu.VMEM((5, 128, 128), F32),
             pltpu.VMEM((960, 128), F32),
             pltpu.VMEM((ORDER, 128), F32),
         ],
         name="solve",
-    )(whole.reshape(PACKED, 128))
-    total = part
-    for bit in (1, 2, 4):
-        total = total + lax.ppermute(total, "fac", [(i, i ^ bit) for i in range(groups)])
-    factor = jnp.sqrt(clip_rate * kernel.size / total[0, 0])
-    update = raw.reshape(TAPS, 16, 128) * factor
-    return (in_grad.reshape(shape), update)
+    )(core, mine, other)
+    every = lax.all_to_all(part, "fac", 0, 0, tiled=True)
+    update = call(
+        functools.partial(scale_kernel, size=kernel.size),
+        jax.ShapeDtypeStruct((ORDER, 128), F32),
+        name="scale",
+    )(raw, every)
+    return (in_grad.reshape(shape), update.reshape(TAPS, 16, 128))
 
 
 def solution(mesh):

time: 153 us -> 139 us (0.908)
  waiting for transfers between devices: 29.4 us -> 16.7 us
  blocking collectives: 63.9 us -> 57 us
  Pallas kernels: 26.6 us -> 30.5 us
  starting transfers between devices: 26.3 us -> 29.9 us
    ppermute x3, starting transfers between devices: 1.32 us -> 11.1 us  [the longest x1 7.83 us: on_device(): lax.ppermute(give, 'fac', [(i, (i + wide) % groups) for i in range(groups)])]
    all_to_all x1, waiting for transfers between devices: 15.9 us -> 7.27 us  [on_device(): every = lax.all_to_all(part, 'fac', 0, 0, tiled=True)]
    ppermute x1, starting transfers between devices: 12.6 us -> 5.62 us  [on_device(): act_prev = lax.ppermute(recv[:, :16, 256:], 'space', up)]
    all_to_all x2 -> x3, blocking collectives: 63.9 us -> 57 us  [the longest x1 22.4 us: on_device(): lax.all_to_all(both.reshape(chips, share, 128), 'space', 0, 0, axis_index...]
    ppermute x3, waiting for transfers between devices: 9.85 us -> 5.8 us  [the longest x1 4.08 us: on_device(): lax.ppermute(give, 'fac', [(i, (i + wide) % groups) for i in range(groups)])]
    pallas_call x4 -> x7, Pallas kernels: 26.6 us -> 30.5 us  [run(): pl.pallas_call(body, out_shape=out_shape, in_specs=[SMEM if a.dtype == jn...]
    all_to_all x1, starting transfers between devices: 4.76 us -> 6.75 us  [on_device(): every = lax.all_to_all(part, 'fac', 0, 0, tiled=True)]
    ppermute x1, starting transfers between devices: 3.54 us -> 1.92 us  [on_device(): cot_prev = lax.ppermute(cot[256:], 'space', up)]
  transfers between devices with their start and end apart: 8 -> 8, of which waited for: 5 -> 4; matrix products, arithmetic and copies ran while one was open for 0% -> 0% of each run, Pallas kernels for 15% -> 19%
where the time goes in v2:
time: 139 us; the launch traced here: 137 us
  blocking collectives  57 us (41%)
  Pallas kernels  30.5 us (22%)
  starting transfers between devices  29.9 us (22%)
  waiting for transfers between devices  16.7 us (12%)
  local copies, waits for them, and re-layouts  1.86 us (1%)
    pallas_call x7, Pallas kernels, run(): pl.pallas_call(body, out_shape=out_shape, in_specs=[SMEM if a.dtype == jn...  30.5 us
    all_to_all x1, blocking collectives, on_device(): lax.all_to_all(both.reshape(chips, share, 128), 'space', 0, 0, axis_index...  22.4 us
    all_to_all x1, blocking collectives, on_device(): lax.all_to_all(send, 'fac', 0, 0, axis_index_groups=along_x, tiled=True)  19.3 us
    all_to_all x1, blocking collectives, on_device(): lax.all_to_all(copies, 'space', 0, 0, axis_index_groups=plane, tiled=True)  15.3 us
    ppermute x1, starting transfers between devices, on_device(): lax.ppermute(give, 'fac', [(i, (i + wide) % groups) for i in range(groups)])  7.83 us
    all_to_all x1, waiting for transfers between devices, on_device(): every = lax.all_to_all(part, 'fac', 0, 0, tiled=True)  7.27 us
    all_to_all x1, starting transfers between devices, on_device(): every = lax.all_to_all(part, 'fac', 0, 0, tiled=True)  6.75 us
    ppermute x1, starting transfers between devices, on_device(): act_prev = lax.ppermute(recv[:, :16, 256:], 'space', up)  5.62 us
  transfers between devices with their start and end apart: 8, of which 4 were waited for; matrix products, arithmetic and copies ran while one was open for 0% of the time, Pallas kernels for 19%

profile of v2, /device:TPU:1, one launch (start us, length us, event | category | flops | bytes accessed | tf_op | source)
XLA Modules:
  0.0 136.8 jit_solution(8266599037724947453)
XLA Ops:
  0.6 0.0 copy-start
  0.7 0.9 copy-done
  1.6 0.9 copy-done.3
  2.5 0.1 prep.1
  2.6 7.8 %collective-permute-start.2 = (bf16[192,512]{1,0:T(8,128)(2,1)S(1)}, bf16[192,512]{1,0:T(8,128)(2,1)S(1)}, u32[]{:S(2)}, u32[]{:S(2)}) collective-permute-start(bf16[192,512]{1,0:T(8,128)(2,1)S(1)} %get-tuple-element.7), channel_id=1, source_target_pairs={{0,4},{1,5},{2,6},{3,7},{4,0},{5,1},{6,2},{7,3},{8,12},{9,13},{10,... | collective-permute-start | bytes 589832 | tf_op jit(solution)/shard_map/ppermute | solution.py:292
  10.4 4.1 %collective-permute-done.2.got_ref = bf16[192,512]{1,0:T(8,128)(2,1)S(1)} collective-permute-done((bf16[192,512]{1,0:T(8,128)(2,1)S(1)}, bf16[192,512]{1,0:T(8,128)(2,1)S(1)}, u32[]{:S(2)}, u32[]{:S(2)}) %collective-permute-start.2) | collective-permute-done | bytes 196640 | tf_op jit(solution)/shard_map/ppermute | solution.py:292
  14.5 0.1 spread.1
  14.6 19.3 %all_to_all.20 = bf16[4,2,144,512]{3,2,1,0:T(8,128)(2,1)S(1)} all-to-all(bf16[4,2,144,512]{3,2,1,0:T(8,128)(2,1)S(1)} %spread.1), channel_id=1, replica_groups={{0,1,2,3},{4,5,6,7},{8,9,10,11},{12,13,14,15},{16,17,18,19},{20,21,22,2..., dimensions={0} | all-to-all | bytes 2359296 | tf_op jit(solution)/shard_map/all_to_all | solution.py:295
  33.9 5.6 %collective-permute-start.3 = (bf16[8,16,256]{2,1,0:T(8,128)(2,1)S(1)}, bf16[8,16,256]{2,1,0:T(8,128)(2,1)S(1)}, u32[]{:S(2)}, u32[]{:S(2)}) collective-permute-start(bf16[8,16,256]{2,1,0:T(8,128)(2,1)S(1)} %get-tuple-element.11), channel_id=1, source_target_pairs={{0,8},{8,16},{16,24},{24,32},{32,40},{40,48},{48,56},{56,64},{64,7... | collective-permute-start | bytes 196616 | tf_op jit(solution)/shard_map/ppermute | solution.py:296
  39.5 1.9 %collective-permute-start.4 = (bf16[8,16,256]{2,1,0:T(8,128)(2,1)S(1)}, bf16[8,16,256]{2,1,0:T(8,128)(2,1)S(1)}, u32[]{:S(2)}, u32[]{:S(2)}) collective-permute-start(bf16[8,16,256]{2,1,0:T(8,128)(2,1)S(1)} %get-tuple-element.10), channel_id=1, source_target_pairs={{8,0},{16,8},{24,16},{32,24},{40,32},{48,40},{56,48},{64,56},{72,6... | collective-permute-start | bytes 196616 | tf_op jit(solution)/shard_map/ppermute | solution.py:297
  41.5 3.6 %collective-permute-done.4.next_ref = bf16[8,16,256]{2,1,0:T(8,128)(2,1)S(1)} collective-permute-done((bf16[8,16,256]{2,1,0:T(8,128)(2,1)S(1)}, bf16[8,16,256]{2,1,0:T(8,128)(2,1)S(1)}, u32[]{:S(2)}, u32[]{:S(2)}) %collective-permute-start.4) | collective-permute-done | bytes 65568 | tf_op jit(solution)/shard_map/ppermute | solution.py:297
  45.1 3.6 %stats.1 = f32[2,768,128]{2,1,0:T(8,128)S(1)} custom-call(s32[1]{0:T(128)} %bitcast.4.core_ref, bf16[8,144,512]{2,1,0:T(8,128)(2,1)S(1)} %bitcast.18, bf16[8,16,256]{2,1,0:T(8,128)(2,1)S(1)} %collective-permute-done.3.prev_ref, bf16[8,16,256]{2,1,0:T(8,128)(2,1)S(1)} %collective-permute-done.4.next_ref), custom_call_target="tpu_custom_call" | custom-call | tf_op jit(solution)/shard_map/stats/pallas_call | solution.py:34
  48.8 0.1 collective-permute-start.5
  48.9 1.7 %collective-permute-done.5 = f32[768,128]{1,0:T(8,128)S(1)} collective-permute-done((f32[768,128]{1,0:T(8,128)S(1)}, f32[768,128]{1,0:T(8,128)S(1)}, u32[]{:S(2)}, u32[]{:S(2)}) %collective-permute-start.5) | collective-permute-done | bytes 393248 | tf_op jit(solution)/shard_map/ppermute | solution.py:317
  50.7 22.4 %all_to_all.21.parts_ref = f32[16,48,128]{2,1,0:T(8,128)S(1)} all-to-all(f32[16,48,128]{2,1,0:T(8,128)S(1)} %bitcast.24), channel_id=1, replica_groups={{0,16,32,48,64,80,96,112,128,144,160,176,192,208,224,240},{8,24,40,56,7..., dimensions={0} | all-to-all | bytes 786432 | tf_op jit(solution)/shard_map/all_to_all | solution.py:318
  73.1 15.3 %all_to_all.22 = f32[16,48,128]{2,1,0:T(8,128)S(1)} all-to-all(f32[16,48,128]{2,1,0:T(8,128)S(1)} %fold.1), channel_id=1, replica_groups={{0,16,32,48,64,80,96,112,128,144,160,176,192,208,224,240},{8,24,40,56,7..., dimensions={0} | all-to-all | bytes 786432 | tf_op jit(solution)/shard_map/all_to_all | solution.py:322
  88.4 3.1 %collective-permute-start.6 = (f32[768,128]{1,0:T(8,128)S(1)}, f32[768,128]{1,0:T(8,128)S(1)}, u32[]{:S(2)}, u32[]{:S(2)}) collective-permute-start(f32[768,128]{1,0:T(8,128)S(1)} %bitcast.19), channel_id=1, source_target_pairs={{0,8},{8,0},{16,24},{24,16},{32,40},{40,32},{48,56},{56,48},{64,72... | collective-permute-start | bytes 1179656 | tf_op jit(solution)/shard_map/ppermute | solution.py:323
  91.6 1.9 %collective-permute-start = (bf16[256,128]{1,0:T(8,128)(2,1)S(1)}, bf16[256,128]{1,0:T(8,128)(2,1)S(1)}, u32[]{:S(2)}, u32[]{:S(2)}) collective-permute-start(bf16[256,128]{1,0:T(8,128)(2,1)S(1)} %bitcast.28), channel_id=1, source_target_pairs={{0,8},{8,16},{16,24},{24,32},{32,40},{40,48},{48,56},{56,64},{64,7... | collective-permute-start | bytes 196616 | tf_op jit(solution)/shard_map/ppermute | solution.py:280
  93.5 2.6 %collective-permute-start.1 = (bf16[256,128]{1,0:T(8,128)(2,1)S(1)}, bf16[256,128]{1,0:T(8,128)(2,1)S(1)}, u32[]{:S(2)}, u32[]{:S(2)}) collective-permute-start(bf16[256,128]{1,0:T(8,128)(2,1)S(1)} %bitcast.27), channel_id=1, source_target_pairs={{8,0},{16,8},{24,16},{32,24},{40,32},{48,40},{56,48},{64,56},{72,6... | collective-permute-start | bytes 196616 | tf_op jit(solution)/shard_map/ppermute | solution.py:281
  96.1 24.1 %solve.1 = (f32[432,128]{1,0:T(8,128)S(1)}, f32[8,8,128]{2,1,0:T(8,128)}) custom-call(s32[1]{0:T(128)} %bitcast.4.core_ref, f32[768,128]{1,0:T(8,128)S(1)} %bitcast.20, f32[768,128]{1,0:T(8,128)S(1)} %collective-permute-done.6.other_ref), custom_call_target="tpu_custom_call" | custom-call | tf_op jit(solution)/shard_map/solve/pallas_call | solution.py:34
  120.2 6.7 %all-to-all-start.3 = ((f32[8,8,128]{2,1,0:T(8,128)}), f32[8,8,128]{2,1,0:T(8,128)S(1)}, u32[]{:S(2)}, u32[]{:S(2)}) async-start(f32[8,8,128]{2,1,0:T(8,128)} %get-tuple-element.9), calls=%async_computation.3 | async-start | bytes 65536 | tf_op jit(solution)/shard_map/all_to_all | solution.py:337
  127.0 1.8 %in_grad.1 = bf16[512,128]{1,0:T(8,128)(2,1)} custom-call(bf16[256,128]{1,0:T(8,128)(2,1)S(1)} %collective-permute-done.prev_ref, bf16[512,128]{1,0:T(8,128)(2,1)S(1)} %bitcast.22, bf16[256,128]{1,0:T(8,128)(2,1)S(1)} %collective-permute-done.1.next_ref, bf16[27,128,128]{2,1,0:T(8,128)(2,1)S(1)} %copy-done.2), custom_call_target="tpu_custom_call" | custom-call | tf_op jit(solution)/shard_map/in_grad/pallas_call | solution.py:34
  128.8 7.3 %all-to-all-done.3.parts_ref = f32[8,8,128]{2,1,0:T(8,128)S(1)} async-done(((f32[8,8,128]{2,1,0:T(8,128)}), f32[8,8,128]{2,1,0:T(8,128)S(1)}, u32[]{:S(2)}, u32[]{:S(2)}) %all-to-all-start.3) | async-done | bytes 32800 | tf_op jit(solution)/shard_map/all_to_all | solution.py:337
  136.0 0.7 scale.1
  (14 shorter events, 0.2 us)
Async XLA Ops:
  0.6 0.9 copy-start
  1.6 0.9 copy-start.3
  2.6 11.9 %collective-permute-start.2 = (bf16[192,512]{1,0:T(8,128)(2,1)S(1)}, bf16[192,512]{1,0:T(8,128)(2,1)S(1)}, u32[]{:S(2)}, u32[]{:S(2)}) collective-permute-start(bf16[192,512]{1,0:T(8,128)(2,1)S(1)} %get-tuple-element.7), channel_id=1, source_target_pairs={{0,4},{1,5},{2,6},{3,7},{4,0},{5,1},{6,2},{7,3},{8,12},{9,13},{10,... | collective-permute-start | bytes 589832 | tf_op jit(solution)/shard_map/ppermute | solution.py:292
  33.9 7.6 %collective-permute-start.3 = (bf16[8,16,256]{2,1,0:T(8,128)(2,1)S(1)}, bf16[8,16,256]{2,1,0:T(8,128)(2,1)S(1)}, u32[]{:S(2)}, u32[]{:S(2)}) collective-permute-start(bf16[8,16,256]{2,1,0:T(8,128)(2,1)S(1)} %get-tuple-element.11), channel_id=1, source_target_pairs={{0,8},{8,16},{16,24},{24,32},{32,40},{40,48},{48,56},{56,64},{64,7... | collective-permute-start | bytes 196616 | tf_op jit(solution)/shard_map/ppermute | solution.py:296
  39.5 5.6 %collective-permute-start.4 = (bf16[8,16,256]{2,1,0:T(8,128)(2,1)S(1)}, bf16[8,16,256]{2,1,0:T(8,128)(2,1)S(1)}, u32[]{:S(2)}, u32[]{:S(2)}) collective-permute-start(bf16[8,16,256]{2,1,0:T(8,128)(2,1)S(1)} %get-tuple-element.10), channel_id=1, source_target_pairs={{8,0},{16,8},{24,16},{32,24},{40,32},{48,40},{56,48},{64,56},{72,6... | collective-permute-start | bytes 196616 | tf_op jit(solution)/shard_map/ppermute | solution.py:297
  48.8 1.8 %collective-permute-start.5 = (f32[768,128]{1,0:T(8,128)S(1)}, f32[768,128]{1,0:T(8,128)S(1)}, u32[]{:S(2)}, u32[]{:S(2)}) collective-permute-start(f32[768,128]{1,0:T(8,128)S(1)} %slice_bitcast_fusion), channel_id=1, source_target_pairs={{0,8},{8,0},{16,24},{24,16},{32,40},{40,32},{48,56},{56,48},{64,72... | collective-permute-start | bytes 1179656 | tf_op jit(solution)/shard_map/ppermute | solution.py:317
  50.6 40.9 %copy-start.1 = (bf16[1,2,16,16,128]{4,3,2,1,0:T(8,128)(2,1)S(1)}, bf16[1,2,16,16,128]{4,3,2,1,0:T(8,128)(2,1)}, u32[]{:S(2)}) copy-start(bf16[1,2,16,16,128]{4,3,2,1,0:T(8,128)(2,1)} %param.4) | copy-start | bytes 393220
  73.1 53.9 %copy-start.2 = (bf16[27,128,128]{2,1,0:T(8,128)(2,1)S(1)}, bf16[27,128,128]{2,1,0:T(8,128)(2,1)}, u32[]{:S(2)}) copy-start(bf16[27,128,128]{2,1,0:T(8,128)(2,1)} %kern_ref.1) | copy-start | bytes 2654212
  88.4 7.7 %collective-permute-start.6 = (f32[768,128]{1,0:T(8,128)S(1)}, f32[768,128]{1,0:T(8,128)S(1)}, u32[]{:S(2)}, u32[]{:S(2)}) collective-permute-start(f32[768,128]{1,0:T(8,128)S(1)} %bitcast.19), channel_id=1, source_target_pairs={{0,8},{8,0},{16,24},{24,16},{32,40},{40,32},{48,56},{56,48},{64,72... | collective-permute-start | bytes 1179656 | tf_op jit(solution)/shard_map/ppermute | solution.py:323
  91.6 35.4 %collective-permute-start = (bf16[256,128]{1,0:T(8,128)(2,1)S(1)}, bf16[256,128]{1,0:T(8,128)(2,1)S(1)}, u32[]{:S(2)}, u32[]{:S(2)}) collective-permute-start(bf16[256,128]{1,0:T(8,128)(2,1)S(1)} %bitcast.28), channel_id=1, source_target_pairs={{0,8},{8,16},{16,24},{24,32},{32,40},{40,48},{48,56},{56,64},{64,7... | collective-permute-start | bytes 196616 | tf_op jit(solution)/shard_map/ppermute | solution.py:280
  93.5 33.5 %collective-permute-start.1 = (bf16[256,128]{1,0:T(8,128)(2,1)S(1)}, bf16[256,128]{1,0:T(8,128)(2,1)S(1)}, u32[]{:S(2)}, u32[]{:S(2)}) collective-permute-start(bf16[256,128]{1,0:T(8,128)(2,1)S(1)} %bitcast.27), channel_id=1, source_target_pairs={{8,0},{16,8},{24,16},{32,24},{40,32},{48,40},{56,48},{64,56},{72,6... | collective-permute-start | bytes 196616 | tf_op jit(solution)/shard_map/ppermute | solution.py:281
  120.2 15.8 %all-to-all-start.3 = ((f32[8,8,128]{2,1,0:T(8,128)}), f32[8,8,128]{2,1,0:T(8,128)S(1)}, u32[]{:S(2)}, u32[]{:S(2)}) async-start(f32[8,8,128]{2,1,0:T(8,128)} %get-tuple-element.9), calls=%async_computation.3 | async-start | bytes 65536 | tf_op jit(solution)/shard_map/all_to_all | solution.py:337

commit v3 on v2

v3 whole, which is shorter than its diff:
```python
import functools
import math

import jax
import jax.numpy as jnp
from jax import lax
from jax.experimental import pallas as pl
from jax.experimental.pallas import tpu as pltpu
from jax.sharding import PartitionSpec as P

damping = 0.1
clip_rate = 0.05
TAPS = 27
F32 = jnp.float32
BF16 = jnp.bfloat16
HI = lax.Precision.HIGHEST
VMEM = pl.BlockSpec(memory_space=pltpu.VMEM)
PARAMS = pltpu.CompilerParams(vmem_limit_bytes=48 * 1024 * 1024)

ORDER = 432
EDGES = (0, 128, 256, 384)
STARTS = (0, 432, 736, 912)
GRAD_AT = 960
COT_AT = 1392
PACKED = 1536
HALF = PACKED // 2
QUARTER = HALF // 4


SMEM = pl.BlockSpec(memory_space=pltpu.SMEM)


def call(body, out_shape, scratch=(), name=None):
    def run(*args):
        return pl.pallas_call(
            body,
            out_shape=out_shape,
            in_specs=[SMEM if a.dtype == jnp.int32 else VMEM for a in args],
            out_specs=jax.tree.map(lambda _: VMEM, out_shape),
            scratch_shapes=list(scratch),
            compiler_params=PARAMS,
            name=name,
        )(*args)

    return run


def nt(a, b, precision=None):
    return lax.dot_general(a, b, (((1,), (1,)), ((), ())), precision=precision, preferred_element_type=F32)


def nn(a, b, precision=None):
    return lax.dot_general(a, b, (((1,), (0,)), ((), ())), precision=precision, preferred_element_type=F32)


def tn(a, b, precision=None):
    return lax.dot_general(a, b, (((0,), (0,)), ((), ())), precision=precision, preferred_element_type=F32)


def prep_kernel(place_ref, act_ref, cot_ref, give_ref, *rest):
    sends, act_t = rest[:-1], rest[-1]
    half = act_ref.shape[1] // 2
    act_t[...] = act_ref[...].astype(F32).T.astype(BF16)
    cot = cot_ref[...].astype(F32).T.astype(BF16)
    high, turn = place_ref[2], place_ref[3]
    give_ref[0:half, :] = act_t[pl.ds(pl.multiple_of((1 - high) * half, half), half), :]
    give_ref[half:, :] = cot
    for k, send_ref in enumerate(sends):
        at = high * half + ((turn + k) % 4) * 16
        send_ref[0:16, :] = act_t[pl.ds(pl.multiple_of(at, 16), 16), :]
        send_ref[16:, :] = cot


def spread_kernel(place_ref, got_ref, *sends):
    half = got_ref.shape[0] - 128
    for k, send_ref in enumerate(sends):
        at = ((place_ref[3] + k) % 4) * 16
        send_ref[0:16, :] = got_ref[pl.ds(pl.multiple_of(at, 16), 16), :]
        send_ref[16:, :] = got_ref[half:, :]


def rim_kernel(*refs):
    parts, (first_ref, last_ref) = refs[:-2], refs[-2:]
    for s, ref in enumerate(parts):
        first_ref[s] = ref[0:16, 0:256]
        last_ref[s] = ref[0:16, 256:]


def in_grad_kernel(prev_ref, cot_ref, next_ref, kern_ref, out_ref, rows_ref, shift_ref):
    rows_ref[8:264, :] = prev_ref[...].astype(F32)
    rows_ref[264:776, :] = cot_ref[...].astype(F32)
    rows_ref[776:1032, :] = next_ref[...].astype(F32)
    z = lax.broadcasted_iota(jnp.int32, (256, 128), 0) % 16
    zeros = jnp.zeros((16, 384), BF16)
    for plane in range(4):
        base = plane * 288
        shift_ref[base : base + 16, :] = zeros
        shift_ref[base + 272 : base + 288, :] = zeros
        for n, c in enumerate((-1, 0, 1)):
            at = 8 + plane * 256 + c
            cells = rows_ref[at : at + 256, :]
            if c:
                cells = jnp.where((z + c >= 0) & (z + c < 16), cells, 0.0)
            shift_ref[base + 16 : base + 272, n * 128 : (n + 1) * 128] = cells.astype(BF16)
    for x in range(2):
        total = jnp.zeros((256, 128), F32)
        for a in (-1, 0, 1):
            for b in (-1, 0, 1):
                for n, c in enumerate((-1, 0, 1)):
                    tap = 9 * (1 - a) + 3 * (1 - b) + (1 - c)
                    at = (x + 1 + a) * 288 + 16 + 16 * b
                    rows = shift_ref[at : at + 256, n * 128 : (n + 1) * 128]
                    total = total + nt(rows, kern_ref[tap])
        out_ref[x * 256 : (x + 1) * 256, :] = total.astype(BF16)


def stats_kernel(place_ref, prev_ref, next_ref, *refs):
    slabs = prev_ref.shape[0]
    parts, (keep_ref, give_ref, x_ref, out_ref) = refs[:slabs], refs[slabs:]
    core, turn = place_ref[0], place_ref[1]
    lane = lax.broadcasted_iota(jnp.int32, (16, 1024), 1)
    y = (lane // 16) % 16
    z = lane % 16
    for s in range(slabs):
        cols = slice(s * 512, (s + 1) * 512)
        planes = jnp.concatenate([prev_ref[s], parts[s][0:16, :], next_ref[s]], axis=1).astype(F32)
        for b in (-1, 0, 1):
            for c in (-1, 0, 1):
                d = 16 * b + c
                moved = planes
                if d:
                    moved = pltpu.roll(planes, (-d) % 1024, 1)
                    ok = (y + b >= 0) & (y + b < 16) & (z + c >= 0) & (z + c < 16)
                    moved = jnp.where(ok, moved, 0.0)
                moved = moved.astype(BF16)
                for a in (-1, 0, 1):
                    tap = 9 * (a + 1) + 3 * (b + 1) + (c + 1)
                    at = (1 + a) * 256
                    x_ref[tap * 16 : (tap + 1) * 16, cols] = moved[:, at : at + 512]
        x_ref[ORDER:, cols] = parts[s][16:, :]
    for edge, start in zip(EDGES, STARTS):
        tile = nt(x_ref[edge:ORDER, :], x_ref[edge : edge + 128, :])
        out_ref[start : start + ORDER - edge, :] = tile
    out_ref[GRAD_AT : GRAD_AT + ORDER + 128, :] = nt(x_ref[...], x_ref[ORDER:, :])
    out_ref[COT_AT + 128 :, :] = jnp.zeros((PACKED - COT_AT - 128, 128), F32)
    for k in range(4):
        for half, ref in ((core, keep_ref), (1 - core, give_ref)):
            at = half * HALF + ((turn + k) % 4) * QUARTER
            ref[k * QUARTER : (k + 1) * QUARTER, :] = out_ref[pl.ds(pl.multiple_of(at, QUARTER), QUARTER), :]


def pair_kernel(keep_ref, got_ref, *outs):
    for k, out_ref in enumerate(outs):
        rows = slice(k * QUARTER, (k + 1) * QUARTER)
        out_ref[...] = keep_ref[rows, :] + got_ref[rows, :]


def fold_kernel(*refs):
    total = refs[0][...]
    for ref in refs[1:-1]:
        total = total + ref[...]
    refs[-1][...] = total


def fold_in_order_kernel(place_ref, *refs):
    parts, out_ref, slots = refs[:4], refs[4], refs[5]
    for k, ref in enumerate(parts):
        slots[(place_ref[4] + 4 - k) % 4] = ref[...]
    out_ref[...] = slots[0] + slots[1] + slots[2] + slots[3]


def scale_kernel(raw_ref, parts_ref, out_ref, *, size):
    total = parts_ref[0]
    for p in range(1, parts_ref.shape[0]):
        total = total + parts_ref[p]
    factor = jnp.sqrt(clip_rate * size / total)[0:1, :]
    out_ref[...] = raw_ref[...] * factor


def spread(row):
    return jnp.broadcast_to(row, (8, 128))


def sweep(tiles, g):
    shape = tiles[g].shape
    lane = lax.broadcasted_iota(jnp.int32, shape, 1)
    sub = lax.broadcasted_iota(jnp.int32, shape, 0)
    rows = tiles[g]

    def column(tile, q):
        return jnp.broadcast_to(tile[:, 8 * g + q : 8 * g + q + 1], shape)

    def row(tile, q):
        return jnp.broadcast_to(tile[q : q + 1, :], shape)

    cols = [column(rows, q) for q in range(8)]
    for k in range(0, 8, 2):
        one, two = cols[k], cols[k + 1]
        a, b, d = row(one, k), row(one, k + 1), row(two, k + 1)
        scale = 1.0 / (a * d - b * b)
        ia, ib, id_ = d * scale, -b * scale, a * scale
        upper, lower = sub == k, sub == k + 1
        for q in range(8):
            if q in (k, k + 1):
                continue
            h, l = row(cols[q], k), row(cols[q], k + 1)
            th, tl = ia * h + ib * l, ib * h + id_ * l
            rest = cols[q] - one * th - two * tl
            cols[q] = jnp.where(upper, th, jnp.where(lower, tl, rest))
        cols[k] = jnp.where(upper, ia, jnp.where(lower, ib, -(one * ia + two * ib)))
        cols[k + 1] = jnp.where(upper, ib, jnp.where(lower, id_, -(one * ib + two * id_)))
    terms = [cols[q] * row(rows, q) for q in range(8)]
    while len(terms) > 1:
        terms = [x + y for x, y in zip(terms[::2], terms[1::2])]
    swept = terms[0]
    for q in range(8):
        swept = jnp.where(lane == 8 * g + q, -cols[q], swept)
    heads = [row(swept, q) for q in range(8)]
    inside = (lane >= 8 * g) & (lane < 8 * g + 8)
    out = []
    for i, old in enumerate(tiles):
        if i == g:
            out.append(swept)
            continue
        new = jnp.where(inside, 0.0, old)
        for q in range(8):
            new = new - column(old, q) * heads[q]
        out.append(new)
    return out


def invert(*mats):
    held = [[m[8 * i : 8 * i + 8] for i in range(m.shape[0] // 8)] for m in mats]
    for g in range(len(held[0])):
        held = [sweep(tiles, g) for tiles in held]
    return [jnp.concatenate([-t for t in tiles], axis=0) for tiles in held]


STEP = 64
STEPS = tuple(range(0, ORDER, STEP))


def packed(col, row, rows):
    tile = col // 128
    at = STARTS[tile] + row - EDGES[tile]
    return slice(at, at + rows)


def forward_kernel(core_ref, *refs, count):
    mine, others = refs[:4], refs[4:8]
    z_ref, y_ref, right_ref, part_ref, stat_ref, d_ref, b_ref = refs[8:]
    core, turn = core_ref[0], core_ref[1]
    for k in range(4):
        for half, ref in ((core, mine[k]), (1 - core, others[k])):
            at = half * HALF + ((turn + 4 - k) % 4) * QUARTER
            stat_ref[pl.ds(pl.multiple_of(at, QUARTER), QUARTER), :] = ref[...]
    eye = (
        lax.broadcasted_iota(jnp.int32, (128, 128), 0) == lax.broadcasted_iota(jnp.int32, (128, 128), 1)
    ).astype(F32)
    for p in range(4):
        edge = EDGES[p]
        head = min(128, ORDER - edge)
        rows = stat_ref[STARTS[p] : STARTS[p] + ORDER - edge, :] / count
        y_ref[STARTS[p] : STARTS[p] + ORDER - edge, :] = rows
        y_ref[STARTS[p] : STARTS[p] + head, :] = rows[:head] + damping * eye[:head]
    b_ref[...] = stat_ref[GRAD_AT : GRAD_AT + ORDER, :] / math.sqrt(count)
    right = stat_ref[COT_AT : COT_AT + 128, :] / count + damping * eye

    side = right[64:, :64]
    for p, edge in enumerate(STEPS):
        size = min(STEP, ORDER - edge)
        half = (edge % 128) // STEP
        lanes = slice(half * STEP, half * STEP + size)
        d = y_ref[packed(edge, edge, size), lanes] if p == 0 else d_ref[0:size, 0:size]
        if p == 0:
            w, r_inv = invert(d, right[:64, :64])
            r_y = nn(side, r_inv, HI)
            r_next = right[64:, 64:] - nt(r_y, side, HI)
        elif p == 1:
            w, t_inv = invert(d, r_next)
            low = -nn(t_inv, r_y, HI)
            top = r_inv - tn(r_y, low, HI)
            inverse = jnp.concatenate(
                [jnp.concatenate([top, low.T], axis=1), jnp.concatenate([low, t_inv], axis=1)], axis=0
            )
            right_ref[...] = inverse
        else:
            (w,) = invert(d)
        z_ref[edge : edge + size, :] = nn(w, b_ref[edge : edge + size, :], HI)
        below = edge + size
        left = ORDER - below
        if left == 0:
            break
        low = y_ref[packed(edge, below, left), lanes]
        y = nn(low, w, HI)
        near = min(STEP, left)
        at = slice((1 - half) * STEP, (1 - half) * STEP + near)
        d_ref[0:near, 0:near] = y_ref[packed(below, below, near), at] - nt(y[:near], low[:near], HI)
        y_ref[packed(edge, below, left), lanes] = y
        b_ref[below:, :] = b_ref[below:, :] - nn(y, b_ref[edge : edge + size, :], HI)
        if half == 0:
            span = packed(edge, below, left)
            y_ref[span, STEP:] = y_ref[span, STEP:] - nt(y, low[:STEP], HI)
        for tile in range(edge // 128 + 1, 4):
            first = EDGES[tile] - below
            wide = min(128, ORDER - EDGES[tile])
            span = slice(STARTS[tile], STARTS[tile] + ORDER - EDGES[tile])
            y_ref[span, 0:wide] = y_ref[span, 0:wide] - nt(y[first:], low[first : first + wide], HI)
    prod = tn(b_ref[...], z_ref[...], HI) * right_ref[...]
    acc = prod[0:8]
    for i in range(1, 16):
        acc = acc + prod[8 * i : 8 * i + 8]
    part_ref[...] = jnp.broadcast_to(jnp.sum(acc).reshape(1, 1, 1), part_ref.shape)


def backward_kernel(z_ref, y_ref, right_ref, raw_ref, x_ref):
    for edge in reversed(STEPS):
        size = min(STEP, ORDER - edge)
        below = edge + size
        x = z_ref[edge : edge + size, :]
        if below < ORDER:
            lanes = slice(edge % 128, edge % 128 + size)
            y = y_ref[packed(edge, below, ORDER - below), lanes]
            x = x - tn(y, x_ref[below:, :], HI)
        x_ref[edge : edge + size, :] = x
    raw_ref[...] = nn(x_ref[...], right_ref[...], HI)


def on_device(activations, out_grad, kernel):
    shape = activations.shape
    spaces = lax.axis_size("space")
    groups = lax.axis_size("fac")
    wide = groups // 2
    act = activations.reshape(512, 128)
    cot = out_grad.reshape(512, 128)

    sp, fa = lax.axis_index("space"), lax.axis_index("fac")
    place = jnp.stack([sp % 2, sp // 2 % 4, fa // wide, fa % wide, sp // 8]).astype(jnp.int32)
    up = [(i, i + 1) for i in range(spaces - 1)]
    down = [(i + 1, i) for i in range(spaces - 1)]
    swap = [(i, i ^ 1) for i in range(spaces)]
    ends = [(i, (i + wide) % groups) for i in range(groups)]

    def ring_x(k):
        return [(i, i // wide * wide + (i + k) % wide) for i in range(groups)]

    def ring_y(k):
        return [(i, i // 8 * 8 + (i // 2 % 4 + k) % 4 * 2 + i % 2) for i in range(spaces)]

    def ring_z(k):
        return [(i, (i // 8 + k) % 4 * 8 + i % 8) for i in range(spaces)]

    def rows(count, width=128, dtype=F32):
        return jax.ShapeDtypeStruct((count, width), dtype)

    part = rows(144, 512, BF16)
    give, *sends = call(
        prep_kernel,
        (rows(192, 512, BF16),) + (part,) * 4,
        scratch=[pltpu.VMEM((128, 512), BF16)],
        name="prep",
    )(place, act, cot)
    got = lax.ppermute(give, "fac", ends)
    own = [sends[0]] + [lax.ppermute(sends[k], "fac", ring_x(k)) for k in (1, 2, 3)]
    cot_prev = lax.ppermute(cot[256:], "space", up)
    cot_next = lax.ppermute(cot[:256], "space", down)
    got, own, cot_prev, cot_next = lax.optimization_barrier((got, own, cot_prev, cot_next))

    sends = call(spread_kernel, (part,) * 4, name="spread")(place, got)
    far = [sends[0]] + [lax.ppermute(sends[k], "fac", ring_x(k)) for k in (1, 2, 3)]
    in_grad = call(
        in_grad_kernel,
        rows(512, 128, BF16),
        scratch=[pltpu.VMEM((1040, 128), F32), pltpu.VMEM((1152, 384), BF16)],
        name="in_grad",
    )(cot_prev, cot, cot_next, kernel)
    far, in_grad = lax.optimization_barrier((far, in_grad))

    parts = own + far
    first, last = call(rim_kernel, (jax.ShapeDtypeStruct((groups, 16, 256), BF16),) * 2, name="rim")(*parts)
    prev = lax.ppermute(last, "space", up)
    following = lax.ppermute(first, "space", down)

    keep, give = call(
        stats_kernel,
        (rows(HALF),) * 2,
        scratch=[pltpu.VMEM((ORDER + 128, groups * 512), BF16), pltpu.VMEM((PACKED, 128), F32)],
        name="stats",
    )(place, prev, following, *parts)

    got = lax.ppermute(give, "space", swap)
    quarters = call(pair_kernel, (rows(QUARTER),) * 4, name="pair")(keep, got)
    over_y = [lax.ppermute(quarters[k], "space", ring_y(k)) for k in (1, 2, 3)]
    mine = call(fold_kernel, rows(QUARTER), name="fold_y")(quarters[0], *over_y)
    over_z = [lax.ppermute(mine, "space", ring_z(k)) for k in (1, 2, 3)]
    mine = call(
        fold_in_order_kernel,
        rows(QUARTER),
        scratch=[pltpu.VMEM((4, QUARTER, 128), F32)],
        name="fold_z",
    )(place, mine, *over_z)
    mine = [mine] + [lax.ppermute(mine, "space", ring_y(k)) for k in (1, 2, 3)]
    others = [lax.ppermute(q, "space", swap) for q in mine]

    z, y, right, total = call(
        functools.partial(forward_kernel, count=float(512 * spaces * groups)),
        (rows(ORDER), rows(GRAD_AT), rows(128), jax.ShapeDtypeStruct((groups, 8, 128), F32)),
        scratch=[pltpu.VMEM((PACKED, 128), F32), pltpu.VMEM((STEP, STEP), F32), pltpu.VMEM((ORDER, 128), F32)],
        name="forward",
    )(place, *mine, *others)
    every = lax.all_to_all(total, "fac", 0, 0, tiled=True)
    raw = call(backward_kernel, rows(ORDER), scratch=[pltpu.VMEM((ORDER, 128), F32)], name="backward")(z, y, right)
    update = call(functools.partial(scale_kernel, size=kernel.size), rows(ORDER), name="scale")(raw, every)
    return (in_grad.reshape(shape), update.reshape(TAPS, 16, 128))


def solution(mesh):
    placed = (P("fac", "space", None, None, None), P("fac", "space", None, None, None), P())
    return jax.shard_map(
        on_device,
        mesh=mesh,
        in_specs=placed,
        out_specs=(P("fac", "space", None, None, None), P(None, "fac", None)),
        check_vma=False,
    )
```

time: 139 us -> 130 us (0.935); the launches traced: 137 us -> 130 us
  blocking collectives: 57 us -> 0 us
  starting transfers between devices: 29.9 us -> 57.7 us
  waiting for transfers between devices: 16.7 us -> 33.7 us
  Pallas kernels: 30.5 us -> 34.8 us
    all_to_all x3 -> x0, blocking collectives: 57 us -> none  [the longest x1 22.4 us: on_device(): lax.all_to_all(both.reshape(chips, share, 128), 'space', 0, 0, axis_index...]
    ppermute x5 -> x23, starting transfers between devices: 18.6 us -> 47.5 us  [the longest x3 9.75 us: on_device(): over_y = [lax.ppermute(quarters[k], 'space', ring_y(k)) for k in (1, 2, 3)]]
    ppermute x5 -> x23, waiting for transfers between devices: 9.43 us -> 21 us  [the longest x3 7.3 us: on_device(): over_z = [lax.ppermute(mine, 'space', ring_z(k)) for k in (1, 2, 3)]]
    pallas_call x7 -> x11, Pallas kernels: 30.5 us -> 34.8 us  [run(): pl.pallas_call(body, out_shape=out_shape, in_specs=[SMEM if a.dtype == jn...]
    ppermute x1, waiting for transfers between devices: 0.01 us -> 4.28 us  [on_device(): cot_next = lax.ppermute(cot[:256], 'space', down)]
    all_to_all x1, starting transfers between devices: 6.75 us -> 3.46 us  [on_device(): every = lax.all_to_all(total, 'fac', 0, 0, tiled=True)]
    ppermute x1, starting transfers between devices: 1.92 us -> 4.89 us  [on_device(): cot_prev = lax.ppermute(cot[256:], 'space', up)]
    unnamed x8 -> x6, local copies, waits for them, and re-layouts: 1.81 us -> 2.82 us
  transfers between devices with their start and end apart: 8 -> 26, of which waited for: 4 -> 13; matrix products, arithmetic and copies ran while one was open for 0% -> 0% of each run, Pallas kernels for 19% -> 3%
where the time goes in v3:
time: 130 us
  starting transfers between devices  57.7 us (44%)
  Pallas kernels  34.8 us (27%)
  waiting for transfers between devices  33.7 us (26%)
  local copies, waits for them, and re-layouts  2.92 us (2%)
    pallas_call x11, Pallas kernels, run(): pl.pallas_call(body, out_shape=out_shape, in_specs=[SMEM if a.dtype == jn...  34.8 us
    ppermute x3, starting transfers between devices, on_device(): over_y = [lax.ppermute(quarters[k], 'space', ring_y(k)) for k in (1, 2, 3)]  9.75 us
    ppermute x6, starting transfers between devices, on_device(): lax.ppermute(sends[k], 'fac', ring_x(k))  8.6 us
    ppermute x4, starting transfers between devices, on_device(): others = [lax.ppermute(q, 'space', swap) for q in mine]  7.84 us
    ppermute x3, waiting for transfers between devices, on_device(): over_z = [lax.ppermute(mine, 'space', ring_z(k)) for k in (1, 2, 3)]  7.3 us
    all_to_all x1, waiting for transfers between devices, on_device(): every = lax.all_to_all(total, 'fac', 0, 0, tiled=True)  7.07 us
    ppermute x1, starting transfers between devices, on_device(): got = lax.ppermute(give, 'fac', ends)  6.91 us
    ppermute x1, starting transfers between devices, on_device(): prev = lax.ppermute(last, 'space', up)  5.2 us
  transfers between devices with their start and end apart: 26, of which 13 were waited for; matrix products, arithmetic and copies ran while one was open for 0% of the time, Pallas kernels for 3%

profile of v3, /device:TPU:1, one launch (start us, length us, event | category | flops | bytes accessed | tf_op | source)
XLA Modules:
  0.0 130.0 jit_solution(13336067566740828596)
XLA Ops:
  3.1 2.1 %collective-permute-start.1 = (bf16[144,512]{1,0:T(8,128)(2,1)S(1)}, bf16[144,512]{1,0:T(8,128)(2,1)S(1)}, u32[]{:S(2)}, u32[]{:S(2)}) collective-permute-start(bf16[144,512]{1,0:T(8,128)(2,1)S(1)} %get-tuple-element.37), channel_id=1, source_target_pairs={{0,1},{1,2},{2,3},{3,0},{4,5},{5,6},{6,7},{7,4},{8,9},{9,10},{10,1... | collective-permute-start | bytes 442376 | tf_op jit(solution)/shard_map/ppermute | solution.py:364
  5.3 2.5 %collective-permute-start.2 = (bf16[144,512]{1,0:T(8,128)(2,1)S(1)}, bf16[144,512]{1,0:T(8,128)(2,1)S(1)}, u32[]{:S(2)}, u32[]{:S(2)}) collective-permute-start(bf16[144,512]{1,0:T(8,128)(2,1)S(1)} %get-tuple-element.38), channel_id=1, source_target_pairs={{0,2},{1,3},{2,0},{3,1},{4,6},{5,7},{6,4},{7,5},{8,10},{9,11},{10,... | collective-permute-start | bytes 442376 | tf_op jit(solution)/shard_map/ppermute | solution.py:364
  8.9 6.9 %collective-permute-start = (bf16[192,512]{1,0:T(8,128)(2,1)S(1)}, bf16[192,512]{1,0:T(8,128)(2,1)S(1)}, u32[]{:S(2)}, u32[]{:S(2)}) collective-permute-start(bf16[192,512]{1,0:T(8,128)(2,1)S(1)} %get-tuple-element.35), channel_id=1, source_target_pairs={{0,4},{1,5},{2,6},{3,7},{4,0},{5,1},{6,2},{7,3},{8,12},{9,13},{10,... | collective-permute-start | bytes 589832 | tf_op jit(solution)/shard_map/ppermute | solution.py:363
  15.8 4.9 %collective-permute-start.4 = (bf16[256,128]{1,0:T(8,128)(2,1)S(1)}, bf16[256,128]{1,0:T(8,128)(2,1)S(1)}, u32[]{:S(2)}, u32[]{:S(2)}) collective-permute-start(bf16[256,128]{1,0:T(8,128)(2,1)S(1)} %bitcast.17), channel_id=1, source_target_pairs={{0,8},{8,16},{16,24},{24,32},{32,40},{40,48},{48,56},{56,64},{64,7... | collective-permute-start | bytes 196616 | tf_op jit(solution)/shard_map/ppermute | solution.py:365
  22.0 1.9 %collective-permute-start.5 = (bf16[256,128]{1,0:T(8,128)(2,1)S(1)}, bf16[256,128]{1,0:T(8,128)(2,1)S(1)}, u32[]{:S(2)}, u32[]{:S(2)}) collective-permute-start(bf16[256,128]{1,0:T(8,128)(2,1)S(1)} %bitcast.16), channel_id=1, source_target_pairs={{8,0},{16,8},{24,16},{32,24},{40,32},{48,40},{56,48},{64,56},{72,6... | collective-permute-start | bytes 196616 | tf_op jit(solution)/shard_map/ppermute | solution.py:366
  23.9 4.3 %collective-permute-done.5.next_ref = bf16[256,128]{1,0:T(8,128)(2,1)S(1)} collective-permute-done((bf16[256,128]{1,0:T(8,128)(2,1)S(1)}, bf16[256,128]{1,0:T(8,128)(2,1)S(1)}, u32[]{:S(2)}, u32[]{:S(2)}) %collective-permute-start.5) | collective-permute-done | bytes 65568 | tf_op jit(solution)/shard_map/ppermute | solution.py:366
  29.8 1.9 %collective-permute-start.8 = (bf16[144,512]{1,0:T(8,128)(2,1)S(1)}, bf16[144,512]{1,0:T(8,128)(2,1)S(1)}, u32[]{:S(2)}, u32[]{:S(2)}) collective-permute-start(bf16[144,512]{1,0:T(8,128)(2,1)S(1)} %get-tuple-element.44), channel_id=1, source_target_pairs={{0,3},{1,0},{2,1},{3,2},{4,7},{5,4},{6,5},{7,6},{8,11},{9,8},{10,9... | collective-permute-start | bytes 442376 | tf_op jit(solution)/shard_map/ppermute | solution.py:370
  37.2 5.2 %collective-permute-start.9 = (bf16[8,16,256]{2,1,0:T(8,128)(2,1)S(1)}, bf16[8,16,256]{2,1,0:T(8,128)(2,1)S(1)}, u32[]{:S(2)}, u32[]{:S(2)}) collective-permute-start(bf16[8,16,256]{2,1,0:T(8,128)(2,1)S(1)} %get-tuple-element.56), channel_id=1, source_target_pairs={{0,8},{8,16},{16,24},{24,32},{32,40},{40,48},{48,56},{56,64},{64,7... | collective-permute-start | bytes 196616 | tf_op jit(solution)/shard_map/ppermute | solution.py:381
  42.4 1.9 %collective-permute-start.10 = (bf16[8,16,256]{2,1,0:T(8,128)(2,1)S(1)}, bf16[8,16,256]{2,1,0:T(8,128)(2,1)S(1)}, u32[]{:S(2)}, u32[]{:S(2)}) collective-permute-start(bf16[8,16,256]{2,1,0:T(8,128)(2,1)S(1)} %get-tuple-element.57), channel_id=1, source_target_pairs={{8,0},{16,8},{24,16},{32,24},{40,32},{48,40},{56,48},{64,56},{72,6... | collective-permute-start | bytes 196616 | tf_op jit(solution)/shard_map/ppermute | solution.py:382
  44.3 3.6 %collective-permute-done.10.next_ref = bf16[8,16,256]{2,1,0:T(8,128)(2,1)S(1)} collective-permute-done((bf16[8,16,256]{2,1,0:T(8,128)(2,1)S(1)}, bf16[8,16,256]{2,1,0:T(8,128)(2,1)S(1)}, u32[]{:S(2)}, u32[]{:S(2)}) %collective-permute-start.10) | collective-permute-done | bytes 65568 | tf_op jit(solution)/shard_map/ppermute | solution.py:382
  48.0 4.3 %stats.1 = (f32[768,128]{1,0:T(8,128)S(1)}, f32[768,128]{1,0:T(8,128)S(1)}) custom-call(s32[5]{0:T(128)S(1)} %stack.23.place_ref.core_ref, bf16[8,16,256]{2,1,0:T(8,128)(2,1)S(1)} %collective-permute-done.9.prev_ref, bf16[8,16,256]{2,1,0:T(8,128)(2,1)S(1)} %collective-permute-done.10.next_ref, bf16[144,512]{1,0:T(8,128)(2,1)S(1)} %get-tuple-element.48.refs_0_, ...), custom_call_target="tpu_custom_call" | custom-call | tf_op jit(solution)/shard_map/stats/pallas_call | solution.py:35
  55.7 8.2 %collective-permute-start.13 = (f32[192,128]{1,0:T(8,128)S(1)}, f32[192,128]{1,0:T(8,128)S(1)}, u32[]{:S(2)}, u32[]{:S(2)}) collective-permute-start(f32[192,128]{1,0:T(8,128)S(1)} %get-tuple-element.62), channel_id=1, source_target_pairs={{0,32},{8,40},{16,48},{24,56},{32,0},{40,8},{48,16},{56,24},{64,96... | collective-permute-start | bytes 294920 | tf_op jit(solution)/shard_map/ppermute | solution.py:393
  63.8 1.9 %collective-permute-done.12.refs_1_ = f32[192,128]{1,0:T(8,128)S(1)} collective-permute-done((f32[192,128]{1,0:T(8,128)S(1)}, f32[192,128]{1,0:T(8,128)S(1)}, u32[]{:S(2)}, u32[]{:S(2)}) %collective-permute-start.12) | collective-permute-done | bytes 98336 | tf_op jit(solution)/shard_map/ppermute | solution.py:393
  65.7 3.0 %collective-permute-done.13.refs_2_ = f32[192,128]{1,0:T(8,128)S(1)} collective-permute-done((f32[192,128]{1,0:T(8,128)S(1)}, f32[192,128]{1,0:T(8,128)S(1)}, u32[]{:S(2)}, u32[]{:S(2)}) %collective-permute-start.13) | collective-permute-done | bytes 98336 | tf_op jit(solution)/shard_map/ppermute | solution.py:393
  69.1 2.2 %collective-permute-start.16 = (f32[192,128]{1,0:T(8,128)S(1)}, f32[192,128]{1,0:T(8,128)S(1)}, u32[]{:S(2)}, u32[]{:S(2)}) collective-permute-start(f32[192,128]{1,0:T(8,128)S(1)} %fold_y.1.refs_0_), channel_id=1, source_target_pairs={{0,128},{8,136},{16,144},{24,152},{32,160},{40,168},{48,176},{56,1... | collective-permute-start | bytes 294920 | tf_op jit(solution)/shard_map/ppermute | solution.py:395
  72.5 6.8 %collective-permute-done.16.refs_2_ = f32[192,128]{1,0:T(8,128)S(1)} collective-permute-done((f32[192,128]{1,0:T(8,128)S(1)}, f32[192,128]{1,0:T(8,128)S(1)}, u32[]{:S(2)}, u32[]{:S(2)}) %collective-permute-start.16) | collective-permute-done | bytes 98336 | tf_op jit(solution)/shard_map/ppermute | solution.py:395
  79.9 3.3 %collective-permute-start.20 = (f32[192,128]{1,0:T(8,128)S(1)}, f32[192,128]{1,0:T(8,128)S(1)}, u32[]{:S(2)}, u32[]{:S(2)}) collective-permute-start(f32[192,128]{1,0:T(8,128)S(1)} %fold_z.1.refs_0_), channel_id=1, source_target_pairs={{0,48},{8,56},{16,0},{24,8},{32,16},{40,24},{48,32},{56,40},{64,11... | collective-permute-start | bytes 294920 | tf_op jit(solution)/shard_map/ppermute | solution.py:402
  83.8 1.9 %collective-permute-start.21 = (f32[192,128]{1,0:T(8,128)S(1)}, f32[192,128]{1,0:T(8,128)S(1)}, u32[]{:S(2)}, u32[]{:S(2)}) collective-permute-start(f32[192,128]{1,0:T(8,128)S(1)} %fold_z.1.refs_0_), channel_id=1, source_target_pairs={{0,8},{8,0},{16,24},{24,16},{32,40},{40,32},{48,56},{56,48},{64,72... | collective-permute-start | bytes 294920 | tf_op jit(solution)/shard_map/ppermute | solution.py:403
  85.7 2.6 %collective-permute-start.24 = (f32[192,128]{1,0:T(8,128)S(1)}, f32[192,128]{1,0:T(8,128)S(1)}, u32[]{:S(2)}, u32[]{:S(2)}) collective-permute-start(f32[192,128]{1,0:T(8,128)S(1)} %collective-permute-done.20.refs_3_), channel_id=1, source_target_pairs={{0,8},{8,0},{16,24},{24,16},{32,40},{40,32},{48,56},{56,48},{64,72... | collective-permute-start | bytes 294920 | tf_op jit(solution)/shard_map/ppermute | solution.py:403
  88.3 2.7 %collective-permute-start.23 = (f32[192,128]{1,0:T(8,128)S(1)}, f32[192,128]{1,0:T(8,128)S(1)}, u32[]{:S(2)}, u32[]{:S(2)}) collective-permute-start(f32[192,128]{1,0:T(8,128)S(1)} %collective-permute-done.19.refs_2_), channel_id=1, source_target_pairs={{0,8},{8,0},{16,24},{24,16},{32,40},{40,32},{48,56},{56,48},{64,72... | collective-permute-start | bytes 294920 | tf_op jit(solution)/shard_map/ppermute | solution.py:403
  92.6 24.2 %forward.1 = (f32[432,128]{1,0:T(8,128)S(1)}, f32[960,128]{1,0:T(8,128)S(1)}, f32[128,128]{1,0:T(8,128)S(1)}, f32[8,8,128]{2,1,0:T(8,128)}) custom-call(s32[5]{0:T(128)S(1)} %stack.23.place_ref.core_ref, f32[192,128]{1,0:T(8,128)S(1)} %fold_z.1.refs_0_, f32[192,128]{1,0:T(8,128)S(1)} %collective-permute-done.18.refs_1_, ...), custom_call_target="tpu_custom_call" | custom-call | tf_op jit(solution)/shard_map/forward/pallas_call | solution.py:35
  116.8 3.5 %all-to-all-start = ((f32[8,8,128]{2,1,0:T(8,128)}), f32[8,8,128]{2,1,0:T(8,128)S(1)}, u32[]{:S(2)}, u32[]{:S(2)}) async-start(f32[8,8,128]{2,1,0:T(8,128)} %get-tuple-element.67), calls=%async_computation | async-start | bytes 65536 | tf_op jit(solution)/shard_map/all_to_all | solution.py:411
  120.3 1.9 %backward.1.raw_ref = f32[432,128]{1,0:T(8,128)S(1)} custom-call(f32[432,128]{1,0:T(8,128)S(1)} %get-tuple-element.64.z_ref, f32[960,128]{1,0:T(8,128)S(1)} %get-tuple-element.65.y_ref, f32[128,128]{1,0:T(8,128)S(1)} %get-tuple-element.66.right_ref), custom_call_target="tpu_custom_call" | custom-call | tf_op jit(solution)/shard_map/backward/pallas_call | solution.py:35
  122.2 7.1 %all-to-all-done.parts_ref = f32[8,8,128]{2,1,0:T(8,128)S(1)} async-done(((f32[8,8,128]{2,1,0:T(8,128)}), f32[8,8,128]{2,1,0:T(8,128)S(1)}, u32[]{:S(2)}, u32[]{:S(2)}) %all-to-all-start) | async-done | bytes 32800 | tf_op jit(solution)/shard_map/all_to_all | solution.py:411
  (47 shorter events, 20.5 us)
Async XLA Ops:
  3.1 25.1 %collective-permute-start.1 = (bf16[144,512]{1,0:T(8,128)(2,1)S(1)}, bf16[144,512]{1,0:T(8,128)(2,1)S(1)}, u32[]{:S(2)}, u32[]{:S(2)}) collective-permute-start(bf16[144,512]{1,0:T(8,128)(2,1)S(1)} %get-tuple-element.37), channel_id=1, source_target_pairs={{0,1},{1,2},{2,3},{3,0},{4,5},{5,6},{6,7},{7,4},{8,9},{9,10},{10,1... | collective-permute-start | bytes 442376 | tf_op jit(solution)/shard_map/ppermute | solution.py:364
  5.3 22.9 %collective-permute-start.2 = (bf16[144,512]{1,0:T(8,128)(2,1)S(1)}, bf16[144,512]{1,0:T(8,128)(2,1)S(1)}, u32[]{:S(2)}, u32[]{:S(2)}) collective-permute-start(bf16[144,512]{1,0:T(8,128)(2,1)S(1)} %get-tuple-element.38), channel_id=1, source_target_pairs={{0,2},{1,3},{2,0},{3,1},{4,6},{5,7},{6,4},{7,5},{8,10},{9,11},{10,... | collective-permute-start | bytes 442376 | tf_op jit(solution)/shard_map/ppermute | solution.py:364
  7.7 20.5 %collective-permute-start.3 = (bf16[144,512]{1,0:T(8,128)(2,1)S(1)}, bf16[144,512]{1,0:T(8,128)(2,1)S(1)}, u32[]{:S(2)}, u32[]{:S(2)}) collective-permute-start(bf16[144,512]{1,0:T(8,128)(2,1)S(1)} %get-tuple-element.39), channel_id=1, source_target_pairs={{0,3},{1,0},{2,1},{3,2},{4,7},{5,4},{6,5},{7,6},{8,11},{9,8},{10,9... | collective-permute-start | bytes 442376 | tf_op jit(solution)/shard_map/ppermute | solution.py:364
  8.9 19.3 %collective-permute-start = (bf16[192,512]{1,0:T(8,128)(2,1)S(1)}, bf16[192,512]{1,0:T(8,128)(2,1)S(1)}, u32[]{:S(2)}, u32[]{:S(2)}) collective-permute-start(bf16[192,512]{1,0:T(8,128)(2,1)S(1)} %get-tuple-element.35), channel_id=1, source_target_pairs={{0,4},{1,5},{2,6},{3,7},{4,0},{5,1},{6,2},{7,3},{8,12},{9,13},{10,... | collective-permute-start | bytes 589832 | tf_op jit(solution)/shard_map/ppermute | solution.py:363
  15.8 6.2 %collective-permute-start.4 = (bf16[256,128]{1,0:T(8,128)(2,1)S(1)}, bf16[256,128]{1,0:T(8,128)(2,1)S(1)}, u32[]{:S(2)}, u32[]{:S(2)}) collective-permute-start(bf16[256,128]{1,0:T(8,128)(2,1)S(1)} %bitcast.17), channel_id=1, source_target_pairs={{0,8},{8,16},{16,24},{24,32},{32,40},{40,48},{48,56},{56,64},{64,7... | collective-permute-start | bytes 196616 | tf_op jit(solution)/shard_map/ppermute | solution.py:365
  22.0 6.2 %collective-permute-start.5 = (bf16[256,128]{1,0:T(8,128)(2,1)S(1)}, bf16[256,128]{1,0:T(8,128)(2,1)S(1)}, u32[]{:S(2)}, u32[]{:S(2)}) collective-permute-start(bf16[256,128]{1,0:T(8,128)(2,1)S(1)} %bitcast.16), channel_id=1, source_target_pairs={{8,0},{16,8},{24,16},{32,24},{40,32},{48,40},{56,48},{64,56},{72,6... | collective-permute-start | bytes 196616 | tf_op jit(solution)/shard_map/ppermute | solution.py:366
  28.8 7.6 %collective-permute-start.6 = (bf16[144,512]{1,0:T(8,128)(2,1)S(1)}, bf16[144,512]{1,0:T(8,128)(2,1)S(1)}, u32[]{:S(2)}, u32[]{:S(2)}) collective-permute-start(bf16[144,512]{1,0:T(8,128)(2,1)S(1)} %get-tuple-element.42), channel_id=1, source_target_pairs={{0,1},{1,2},{2,3},{3,0},{4,5},{5,6},{6,7},{7,4},{8,9},{9,10},{10,1... | collective-permute-start | bytes 442376 | tf_op jit(solution)/shard_map/ppermute | solution.py:370
  29.2 7.2 %collective-permute-start.7 = (bf16[144,512]{1,0:T(8,128)(2,1)S(1)}, bf16[144,512]{1,0:T(8,128)(2,1)S(1)}, u32[]{:S(2)}, u32[]{:S(2)}) collective-permute-start(bf16[144,512]{1,0:T(8,128)(2,1)S(1)} %get-tuple-element.43), channel_id=1, source_target_pairs={{0,2},{1,3},{2,0},{3,1},{4,6},{5,7},{6,4},{7,5},{8,10},{9,11},{10,... | collective-permute-start | bytes 442376 | tf_op jit(solution)/shard_map/ppermute | solution.py:370
  29.8 7.4 %collective-permute-start.8 = (bf16[144,512]{1,0:T(8,128)(2,1)S(1)}, bf16[144,512]{1,0:T(8,128)(2,1)S(1)}, u32[]{:S(2)}, u32[]{:S(2)}) collective-permute-start(bf16[144,512]{1,0:T(8,128)(2,1)S(1)} %get-tuple-element.44), channel_id=1, source_target_pairs={{0,3},{1,0},{2,1},{3,2},{4,7},{5,4},{6,5},{7,6},{8,11},{9,8},{10,9... | collective-permute-start | bytes 442376 | tf_op jit(solution)/shard_map/ppermute | solution.py:370
  37.2 7.1 %collective-permute-start.9 = (bf16[8,16,256]{2,1,0:T(8,128)(2,1)S(1)}, bf16[8,16,256]{2,1,0:T(8,128)(2,1)S(1)}, u32[]{:S(2)}, u32[]{:S(2)}) collective-permute-start(bf16[8,16,256]{2,1,0:T(8,128)(2,1)S(1)} %get-tuple-element.56), channel_id=1, source_target_pairs={{0,8},{8,16},{16,24},{24,32},{32,40},{40,48},{48,56},{56,64},{64,7... | collective-permute-start | bytes 196616 | tf_op jit(solution)/shard_map/ppermute | solution.py:381
  42.4 5.6 %collective-permute-start.10 = (bf16[8,16,256]{2,1,0:T(8,128)(2,1)S(1)}, bf16[8,16,256]{2,1,0:T(8,128)(2,1)S(1)}, u32[]{:S(2)}, u32[]{:S(2)}) collective-permute-start(bf16[8,16,256]{2,1,0:T(8,128)(2,1)S(1)} %get-tuple-element.57), channel_id=1, source_target_pairs={{8,0},{16,8},{24,16},{32,24},{40,32},{48,40},{56,48},{64,56},{72,6... | collective-permute-start | bytes 196616 | tf_op jit(solution)/shard_map/ppermute | solution.py:382
  54.1 11.6 %collective-permute-start.12 = (f32[192,128]{1,0:T(8,128)S(1)}, f32[192,128]{1,0:T(8,128)S(1)}, u32[]{:S(2)}, u32[]{:S(2)}) collective-permute-start(f32[192,128]{1,0:T(8,128)S(1)} %get-tuple-element.61), channel_id=1, source_target_pairs={{0,16},{8,24},{16,32},{24,40},{32,48},{40,56},{48,0},{56,8},{64,80... | collective-permute-start | bytes 294920 | tf_op jit(solution)/shard_map/ppermute | solution.py:393
  55.7 13.1 %collective-permute-start.13 = (f32[192,128]{1,0:T(8,128)S(1)}, f32[192,128]{1,0:T(8,128)S(1)}, u32[]{:S(2)}, u32[]{:S(2)}) collective-permute-start(f32[192,128]{1,0:T(8,128)S(1)} %get-tuple-element.62), channel_id=1, source_target_pairs={{0,32},{8,40},{16,48},{24,56},{32,0},{40,8},{48,16},{56,24},{64,96... | collective-permute-start | bytes 294920 | tf_op jit(solution)/shard_map/ppermute | solution.py:393
  63.8 4.9 %collective-permute-start.14 = (f32[192,128]{1,0:T(8,128)S(1)}, f32[192,128]{1,0:T(8,128)S(1)}, u32[]{:S(2)}, u32[]{:S(2)}) collective-permute-start(f32[192,128]{1,0:T(8,128)S(1)} %get-tuple-element.63), channel_id=1, source_target_pairs={{0,48},{8,56},{16,0},{24,8},{32,16},{40,24},{48,32},{56,40},{64,11... | collective-permute-start | bytes 294920 | tf_op jit(solution)/shard_map/ppermute | solution.py:393
  68.8 3.7 %collective-permute-start.17 = (f32[192,128]{1,0:T(8,128)S(1)}, f32[192,128]{1,0:T(8,128)S(1)}, u32[]{:S(2)}, u32[]{:S(2)}) collective-permute-start(f32[192,128]{1,0:T(8,128)S(1)} %fold_y.1.refs_0_), channel_id=1, source_target_pairs={{0,192},{8,200},{16,208},{24,216},{32,224},{40,232},{48,240},{56,2... | collective-permute-start | bytes 294920 | tf_op jit(solution)/shard_map/ppermute | solution.py:395
  69.1 10.2 %collective-permute-start.16 = (f32[192,128]{1,0:T(8,128)S(1)}, f32[192,128]{1,0:T(8,128)S(1)}, u32[]{:S(2)}, u32[]{:S(2)}) collective-permute-start(f32[192,128]{1,0:T(8,128)S(1)} %fold_y.1.refs_0_), channel_id=1, source_target_pairs={{0,128},{8,136},{16,144},{24,152},{32,160},{40,168},{48,176},{56,1... | collective-permute-start | bytes 294920 | tf_op jit(solution)/shard_map/ppermute | solution.py:395
  71.4 7.9 %collective-permute-start.15 = (f32[192,128]{1,0:T(8,128)S(1)}, f32[192,128]{1,0:T(8,128)S(1)}, u32[]{:S(2)}, u32[]{:S(2)}) collective-permute-start(f32[192,128]{1,0:T(8,128)S(1)} %fold_y.1.refs_0_), channel_id=1, source_target_pairs={{0,64},{8,72},{16,80},{24,88},{32,96},{40,104},{48,112},{56,120},{... | collective-permute-start | bytes 294920 | tf_op jit(solution)/shard_map/ppermute | solution.py:395
  79.9 5.8 %collective-permute-start.20 = (f32[192,128]{1,0:T(8,128)S(1)}, f32[192,128]{1,0:T(8,128)S(1)}, u32[]{:S(2)}, u32[]{:S(2)}) collective-permute-start(f32[192,128]{1,0:T(8,128)S(1)} %fold_z.1.refs_0_), channel_id=1, source_target_pairs={{0,48},{8,56},{16,0},{24,8},{32,16},{40,24},{48,32},{56,40},{64,11... | collective-permute-start | bytes 294920 | tf_op jit(solution)/shard_map/ppermute | solution.py:402
  83.1 5.2 %collective-permute-start.19 = (f32[192,128]{1,0:T(8,128)S(1)}, f32[192,128]{1,0:T(8,128)S(1)}, u32[]{:S(2)}, u32[]{:S(2)}) collective-permute-start(f32[192,128]{1,0:T(8,128)S(1)} %fold_z.1.refs_0_), channel_id=1, source_target_pairs={{0,32},{8,40},{16,48},{24,56},{32,0},{40,8},{48,16},{56,24},{64,96... | collective-permute-start | bytes 294920 | tf_op jit(solution)/shard_map/ppermute | solution.py:402
  83.1 7.9 %collective-permute-start.18 = (f32[192,128]{1,0:T(8,128)S(1)}, f32[192,128]{1,0:T(8,128)S(1)}, u32[]{:S(2)}, u32[]{:S(2)}) collective-permute-start(f32[192,128]{1,0:T(8,128)S(1)} %fold_z.1.refs_0_), channel_id=1, source_target_pairs={{0,16},{8,24},{16,32},{24,40},{32,48},{40,56},{48,0},{56,8},{64,80... | collective-permute-start | bytes 294920 | tf_op jit(solution)/shard_map/ppermute | solution.py:402
  83.8 7.9 %collective-permute-start.21 = (f32[192,128]{1,0:T(8,128)S(1)}, f32[192,128]{1,0:T(8,128)S(1)}, u32[]{:S(2)}, u32[]{:S(2)}) collective-permute-start(f32[192,128]{1,0:T(8,128)S(1)} %fold_z.1.refs_0_), channel_id=1, source_target_pairs={{0,8},{8,0},{16,24},{24,16},{32,40},{40,32},{48,56},{56,48},{64,72... | collective-permute-start | bytes 294920 | tf_op jit(solution)/shard_map/ppermute | solution.py:403
  85.7 6.0 %collective-permute-start.24 = (f32[192,128]{1,0:T(8,128)S(1)}, f32[192,128]{1,0:T(8,128)S(1)}, u32[]{:S(2)}, u32[]{:S(2)}) collective-permute-start(f32[192,128]{1,0:T(8,128)S(1)} %collective-permute-done.20.refs_3_), channel_id=1, source_target_pairs={{0,8},{8,0},{16,24},{24,16},{32,40},{40,32},{48,56},{56,48},{64,72... | collective-permute-start | bytes 294920 | tf_op jit(solution)/shard_map/ppermute | solution.py:403
  88.3 3.7 %collective-permute-start.23 = (f32[192,128]{1,0:T(8,128)S(1)}, f32[192,128]{1,0:T(8,128)S(1)}, u32[]{:S(2)}, u32[]{:S(2)}) collective-permute-start(f32[192,128]{1,0:T(8,128)S(1)} %collective-permute-done.19.refs_2_), channel_id=1, source_target_pairs={{0,8},{8,0},{16,24},{24,16},{32,40},{40,32},{48,56},{56,48},{64,72... | collective-permute-start | bytes 294920 | tf_op jit(solution)/shard_map/ppermute | solution.py:403
  116.8 12.5 %all-to-all-start = ((f32[8,8,128]{2,1,0:T(8,128)}), f32[8,8,128]{2,1,0:T(8,128)S(1)}, u32[]{:S(2)}, u32[]{:S(2)}) async-start(f32[8,8,128]{2,1,0:T(8,128)} %get-tuple-element.67), calls=%async_computation | async-start | bytes 65536 | tf_op jit(solution)/shard_map/all_to_all | solution.py:411
  (5 other events, 6.4 us)

commit v4 on v3

--- a/solution.py
+++ b/solution.py
@@ -82,14 +82,16 @@
 def rim_kernel(*refs):
     parts, (first_ref, last_ref) = refs[:-2], refs[-2:]
     for s, ref in enumerate(parts):
-        first_ref[s] = ref[0:16, 0:256]
-        last_ref[s] = ref[0:16, 256:]
+        first_ref[16 * s : 16 * s + 16, :] = ref[0:16, 0:256]
+        last_ref[16 * s : 16 * s + 16, :] = ref[0:16, 256:]
+    first_ref[128:, :] = parts[0][16:, 0:256]
+    last_ref[128:, :] = parts[0][16:, 256:]
 
 
 def in_grad_kernel(prev_ref, cot_ref, next_ref, kern_ref, out_ref, rows_ref, shift_ref):
-    rows_ref[8:264, :] = prev_ref[...].astype(F32)
+    rows_ref[8:264, :] = prev_ref[128:, :].astype(F32).T
     rows_ref[264:776, :] = cot_ref[...].astype(F32)
-    rows_ref[776:1032, :] = next_ref[...].astype(F32)
+    rows_ref[776:1032, :] = next_ref[128:, :].astype(F32).T
     z = lax.broadcasted_iota(jnp.int32, (256, 128), 0) % 16
     zeros = jnp.zeros((16, 384), BF16)
     for plane in range(4):
@@ -114,8 +116,7 @@
         out_ref[x * 256 : (x + 1) * 256, :] = total.astype(BF16)
 
 
-def stats_kernel(place_ref, prev_ref, next_ref, *refs):
-    slabs = prev_ref.shape[0]
+def stats_kernel(place_ref, prev_ref, next_ref, *refs, slabs):
     parts, (keep_ref, give_ref, x_ref, out_ref) = refs[:slabs], refs[slabs:]
     core, turn = place_ref[0], place_ref[1]
     lane = lax.broadcasted_iota(jnp.int32, (16, 1024), 1)
@@ -123,7 +124,8 @@
     z = lane % 16
     for s in range(slabs):
         cols = slice(s * 512, (s + 1) * 512)
-        planes = jnp.concatenate([prev_ref[s], parts[s][0:16, :], next_ref[s]], axis=1).astype(F32)
+        rim = slice(16 * s, 16 * s + 16)
+        planes = jnp.concatenate([prev_ref[rim, :], parts[s][0:16, :], next_ref[rim, :]], axis=1).astype(F32)
         for b in (-1, 0, 1):
             for c in (-1, 0, 1):
                 d = 16 * b + c
@@ -229,10 +231,14 @@
     return out
 
 
-def invert(*mats):
+def invert(mats, beside):
     held = [[m[8 * i : 8 * i + 8] for i in range(m.shape[0] // 8)] for m in mats]
     for g in range(len(held[0])):
         held = [sweep(tiles, g) for tiles in held]
+        if beside:
+            beside.pop(0)()
+    while beside:
+        beside.pop(0)()
     return [jnp.concatenate([-t for t in tiles], axis=0) for tiles in held]
 
 
@@ -248,7 +254,7 @@
 
 def forward_kernel(core_ref, *refs, count):
     mine, others = refs[:4], refs[4:8]
-    z_ref, y_ref, right_ref, part_ref, stat_ref, d_ref, b_ref = refs[8:]
+    z_ref, y_ref, right_ref, part_ref, stat_ref, b_ref = refs[8:]
     core, turn = core_ref[0], core_ref[1]
     for k in range(4):
         for half, ref in ((core, mine[k]), (1 - core, others[k])):
@@ -267,46 +273,78 @@
     right = stat_ref[COT_AT : COT_AT + 128, :] / count + damping * eye
 
     side = right[64:, :64]
+    held = {}
+
+    def first_half():
+        held["y"] = nn(side, held["r"], HI)
+        held["t"] = right[64:, 64:] - nt(held["y"], side, HI)
+
+    def second_half():
+        low = -nn(held["t"], held["y"], HI)
+        top = held["r"] - tn(held["y"], low, HI)
+        right_ref[0:64, 0:64] = top
+        right_ref[0:64, 64:] = low.T
+        right_ref[64:, 0:64] = low
+        right_ref[64:, 64:] = held["t"]
+
+    def first_rows():
+        done = STEPS[-1]
+        held["sum"] = tn(b_ref[0:done, :], z_ref[0:done, :], HI)
+
+    beside = []
+    d = y_ref[packed(0, 0, STEP), 0:STEP]
     for p, edge in enumerate(STEPS):
         size = min(STEP, ORDER - edge)
         half = (edge % 128) // STEP
         lanes = slice(half * STEP, half * STEP + size)
-        d = y_ref[packed(edge, edge, size), lanes] if p == 0 else d_ref[0:size, 0:size]
-        if p == 0:
-            w, r_inv = invert(d, right[:64, :64])
-            r_y = nn(side, r_inv, HI)
-            r_next = right[64:, 64:] - nt(r_y, side, HI)
-        elif p == 1:
-            w, t_inv = invert(d, r_next)
-            low = -nn(t_inv, r_y, HI)
-            top = r_inv - tn(r_y, low, HI)
-            inverse = jnp.concatenate(
-                [jnp.concatenate([top, low.T], axis=1), jnp.concatenate([low, t_inv], axis=1)], axis=0
-            )
-            right_ref[...] = inverse
-        else:
-            (w,) = invert(d)
-        z_ref[edge : edge + size, :] = nn(w, b_ref[edge : edge + size, :], HI)
         below = edge + size
         left = ORDER - below
         if left == 0:
+            beside.append(first_rows)
+        if p == 0:
+            w, held["r"] = invert([d, right[:64, :64]], beside)
+            first_half()
+        elif p == 1:
+            w, held["t"] = invert([d, held["t"]], beside)
+            beside.append(second_half)
+        else:
+            (w,) = invert([d], beside)
+        if left == 0:
+            z = nn(w, b_ref[edge:, :], HI)
+            z_ref[edge:, :] = z
+            held["sum"] = held["sum"] + tn(b_ref[edge:, :], z, HI)
             break
         low = y_ref[packed(edge, below, left), lanes]
-        y = nn(low, w, HI)
         near = min(STEP, left)
         at = slice((1 - half) * STEP, (1 - half) * STEP + near)
-        d_ref[0:near, 0:near] = y_ref[packed(below, below, near), at] - nt(y[:near], low[:near], HI)
-        y_ref[packed(edge, below, left), lanes] = y
-        b_ref[below:, :] = b_ref[below:, :] - nn(y, b_ref[edge : edge + size, :], HI)
-        if half == 0:
+        y_near = nn(low[:near], w, HI)
+        d = y_ref[packed(below, below, near), at] - nt(y_near, low[:near], HI)
+
+        def scale_rows(w=w, low=low, edge=edge, below=below, left=left, lanes=lanes):
+            held["y_now"] = nn(low, w, HI)
+            y_ref[packed(edge, below, left), lanes] = held["y_now"]
+
+        def into_rhs(w=w, edge=edge, size=size, below=below):
+            now = b_ref[edge : edge + size, :]
+            z_ref[edge : edge + size, :] = nn(w, now, HI)
+            b_ref[below:, :] = b_ref[below:, :] - nn(held["y_now"], now, HI)
+
+        def into_half(low=low, edge=edge, below=below, left=left):
             span = packed(edge, below, left)
-            y_ref[span, STEP:] = y_ref[span, STEP:] - nt(y, low[:STEP], HI)
-        for tile in range(edge // 128 + 1, 4):
+            y_ref[span, STEP:] = y_ref[span, STEP:] - nt(held["y_now"], low[:STEP], HI)
+
+        def into_tile(tile, low=low, below=below):
             first = EDGES[tile] - below
             wide = min(128, ORDER - EDGES[tile])
             span = slice(STARTS[tile], STARTS[tile] + ORDER - EDGES[tile])
-            y_ref[span, 0:wide] = y_ref[span, 0:wide] - nt(y[first:], low[first : first + wide], HI)
-    prod = tn(b_ref[...], z_ref[...], HI) * right_ref[...]
+            y_ref[span, 0:wide] = y_ref[span, 0:wide] - nt(held["y_now"][first:], low[first : first + wide], HI)
+
+        beside.append(scale_rows)
+        if half == 0:
+            beside.append(into_half)
+        beside += [functools.partial(into_tile, tile) for tile in range(edge // 128 + 1, 4)]
+        beside.append(into_rhs)
+    prod = held["sum"] * right_ref[...]
     acc = prod[0:8]
     for i in range(1, 16):
         acc = acc + prod[8 * i : 8 * i + 8]
@@ -362,35 +400,33 @@
     )(place, act, cot)
     got = lax.ppermute(give, "fac", ends)
     own = [sends[0]] + [lax.ppermute(sends[k], "fac", ring_x(k)) for k in (1, 2, 3)]
-    cot_prev = lax.ppermute(cot[256:], "space", up)
-    cot_next = lax.ppermute(cot[:256], "space", down)
-    got, own, cot_prev, cot_next = lax.optimization_barrier((got, own, cot_prev, cot_next))
+    got, own = lax.optimization_barrier((got, own))
 
     sends = call(spread_kernel, (part,) * 4, name="spread")(place, got)
     far = [sends[0]] + [lax.ppermute(sends[k], "fac", ring_x(k)) for k in (1, 2, 3)]
+    parts = own + far
+
+    first, last = call(rim_kernel, (rows(256, 256, BF16),) * 2, name="rim")(*parts)
+    prev = lax.ppermute(last, "space", up)
+    following = lax.ppermute(first, "space", down)
+
+    keep, give = call(
+        functools.partial(stats_kernel, slabs=groups),
+        (rows(HALF),) * 2,
+        scratch=[pltpu.VMEM((ORDER + 128, groups * 512), BF16), pltpu.VMEM((PACKED, 128), F32)],
+        name="stats",
+    )(place, prev, following, *parts)
     in_grad = call(
         in_grad_kernel,
         rows(512, 128, BF16),
         scratch=[pltpu.VMEM((1040, 128), F32), pltpu.VMEM((1152, 384), BF16)],
         name="in_grad",
-    )(cot_prev, cot, cot_next, kernel)
-    far, in_grad = lax.optimization_barrier((far, in_grad))
-
-    parts = own + far
-    first, last = call(rim_kernel, (jax.ShapeDtypeStruct((groups, 16, 256), BF16),) * 2, name="rim")(*parts)
-    prev = lax.ppermute(last, "space", up)
-    following = lax.ppermute(first, "space", down)
-
-    keep, give = call(
-        stats_kernel,
-        (rows(HALF),) * 2,
-        scratch=[pltpu.VMEM((ORDER + 128, groups * 512), BF16), pltpu.VMEM((PACKED, 128), F32)],
-        name="stats",
-    )(place, prev, following, *parts)
+    )(prev, cot, following, kernel)
 
     got = lax.ppermute(give, "space", swap)
     quarters = call(pair_kernel, (rows(QUARTER),) * 4, name="pair")(keep, got)
     over_y = [lax.ppermute(quarters[k], "space", ring_y(k)) for k in (1, 2, 3)]
+    over_y, in_grad = lax.optimization_barrier((over_y, in_grad))
     mine = call(fold_kernel, rows(QUARTER), name="fold_y")(quarters[0], *over_y)
     over_z = [lax.ppermute(mine, "space", ring_z(k)) for k in (1, 2, 3)]
     mine = call(
@@ -405,7 +441,7 @@
     z, y, right, total = call(
         functools.partial(forward_kernel, count=float(512 * spaces * groups)),
         (rows(ORDER), rows(GRAD_AT), rows(128), jax.ShapeDtypeStruct((groups, 8, 128), F32)),
-        scratch=[pltpu.VMEM((PACKED, 128), F32), pltpu.VMEM((STEP, STEP), F32), pltpu.VMEM((ORDER, 128), F32)],
+        scratch=[pltpu.VMEM((PACKED, 128), F32), pltpu.VMEM((ORDER, 128), F32)],
         name="forward",
     )(place, *mine, *others)
     every = lax.all_to_all(total, "fac", 0, 0, tiled=True)

time: 130 us -> 124 us (0.954)
  starting transfers between devices: 57.7 us -> 52 us
    ppermute x6, waiting for transfers between devices: 2.53 us -> 9.78 us  [on_device(): lax.ppermute(sends[k], 'fac', ring_x(k))]
    ppermute x2 -> x0, starting transfers between devices: 6.79 us -> none  [the longest x1 4.89 us: on_device(): cot_prev = lax.ppermute(cot[256:], 'space', up)]
    ppermute x2 -> x0, waiting for transfers between devices: 5.59 us -> none  [the longest x1 4.28 us: on_device(): cot_next = lax.ppermute(cot[:256], 'space', down)]
    ppermute x3, starting transfers between devices: 9.75 us -> 5.21 us  [on_device(): over_y = [lax.ppermute(quarters[k], 'space', ring_y(k)) for k in (1, 2, 3)]]
    all_to_all x1, starting transfers between devices: 3.46 us -> 7.23 us  [on_device(): every = lax.all_to_all(total, 'fac', 0, 0, tiled=True)]
    ppermute x3, waiting for transfers between devices: 4.89 us -> 3.03 us  [on_device(): over_y = [lax.ppermute(quarters[k], 'space', ring_y(k)) for k in (1, 2, 3)]]
  transfers between devices with their start and end apart: 26 -> 24, of which waited for: 13 -> 11; matrix products, arithmetic and copies ran while one was open for 0% -> 0% of each run, Pallas kernels for 3% -> 3%
where the time goes in v4:
time: 124 us
  starting transfers between devices  52 us (42%)
  Pallas kernels  35.1 us (28%)
  waiting for transfers between devices  34.3 us (28%)
  local copies, waits for them, and re-layouts  1.75 us (1%)
    pallas_call x11, Pallas kernels, run(): pl.pallas_call(body, out_shape=out_shape, in_specs=[SMEM if a.dtype == jn...  35.1 us
    ppermute x6, waiting for transfers between devices, on_device(): lax.ppermute(sends[k], 'fac', ring_x(k))  9.78 us
    ppermute x6, starting transfers between devices, on_device(): lax.ppermute(sends[k], 'fac', ring_x(k))  9.07 us
    ppermute x4, starting transfers between devices, on_device(): others = [lax.ppermute(q, 'space', swap) for q in mine]  8.13 us
    ppermute x1, starting transfers between devices, on_device(): got = lax.ppermute(give, 'fac', ends)  7.83 us
    ppermute x3, waiting for transfers between devices, on_device(): over_z = [lax.ppermute(mine, 'space', ring_z(k)) for k in (1, 2, 3)]  7.4 us
    all_to_all x1, starting transfers between devices, on_device(): every = lax.all_to_all(total, 'fac', 0, 0, tiled=True)  7.23 us
    all_to_all x1, waiting for transfers between devices, on_device(): every = lax.all_to_all(total, 'fac', 0, 0, tiled=True)  7.07 us
  transfers between devices with their start and end apart: 24, of which 11 were waited for; matrix products, arithmetic and copies ran while one was open for 0% of the time, Pallas kernels for 3%

profile of v4, /device:TPU:1, one launch (start us, length us, event | category | flops | bytes accessed | tf_op | source)
XLA Modules:
  0.0 123.9 jit_solution(18196048036452939576)
XLA Ops:
  3.1 7.8 %collective-permute-start = (bf16[192,512]{1,0:T(8,128)(2,1)S(1)}, bf16[192,512]{1,0:T(8,128)(2,1)S(1)}, u32[]{:S(2)}, u32[]{:S(2)}) collective-permute-start(bf16[192,512]{1,0:T(8,128)(2,1)S(1)} %get-tuple-element.32), channel_id=1, source_target_pairs={{0,4},{1,5},{2,6},{3,7},{4,0},{5,1},{6,2},{7,3},{8,12},{9,13},{10,... | collective-permute-start | bytes 589832 | tf_op jit(solution)/shard_map/ppermute | solution.py:401
  12.2 2.5 %collective-permute-start.2 = (bf16[144,512]{1,0:T(8,128)(2,1)S(1)}, bf16[144,512]{1,0:T(8,128)(2,1)S(1)}, u32[]{:S(2)}, u32[]{:S(2)}) collective-permute-start(bf16[144,512]{1,0:T(8,128)(2,1)S(1)} %get-tuple-element.35), channel_id=1, source_target_pairs={{0,2},{1,3},{2,0},{3,1},{4,6},{5,7},{6,4},{7,5},{8,10},{9,11},{10,... | collective-permute-start | bytes 442376 | tf_op jit(solution)/shard_map/ppermute | solution.py:402
  16.6 4.1 %collective-permute-done.2.refs_2_ = bf16[144,512]{1,0:T(8,128)(2,1)S(1)} collective-permute-done((bf16[144,512]{1,0:T(8,128)(2,1)S(1)}, bf16[144,512]{1,0:T(8,128)(2,1)S(1)}, u32[]{:S(2)}, u32[]{:S(2)}) %collective-permute-start.2) | collective-permute-done | bytes 147488 | tf_op jit(solution)/shard_map/ppermute | solution.py:402
  21.3 1.8 %collective-permute-start.4 = (bf16[144,512]{1,0:T(8,128)(2,1)S(1)}, bf16[144,512]{1,0:T(8,128)(2,1)S(1)}, u32[]{:S(2)}, u32[]{:S(2)}) collective-permute-start(bf16[144,512]{1,0:T(8,128)(2,1)S(1)} %get-tuple-element.43), channel_id=1, source_target_pairs={{0,1},{1,2},{2,3},{3,0},{4,5},{5,6},{6,7},{7,4},{8,9},{9,10},{10,1... | collective-permute-start | bytes 442376 | tf_op jit(solution)/shard_map/ppermute | solution.py:406
  23.1 2.0 %collective-permute-start.5 = (bf16[144,512]{1,0:T(8,128)(2,1)S(1)}, bf16[144,512]{1,0:T(8,128)(2,1)S(1)}, u32[]{:S(2)}, u32[]{:S(2)}) collective-permute-start(bf16[144,512]{1,0:T(8,128)(2,1)S(1)} %get-tuple-element.44), channel_id=1, source_target_pairs={{0,2},{1,3},{2,0},{3,1},{4,6},{5,7},{6,4},{7,5},{8,10},{9,11},{10,... | collective-permute-start | bytes 442376 | tf_op jit(solution)/shard_map/ppermute | solution.py:406
  26.6 3.8 %collective-permute-done.5.refs_6_ = bf16[144,512]{1,0:T(8,128)(2,1)S(1)} collective-permute-done((bf16[144,512]{1,0:T(8,128)(2,1)S(1)}, bf16[144,512]{1,0:T(8,128)(2,1)S(1)}, u32[]{:S(2)}, u32[]{:S(2)}) %collective-permute-start.5) | collective-permute-done | bytes 147488 | tf_op jit(solution)/shard_map/ppermute | solution.py:406
  30.4 5.7 %collective-permute-start.7 = (bf16[256,256]{1,0:T(8,128)(2,1)S(1)}, bf16[256,256]{1,0:T(8,128)(2,1)S(1)}, u32[]{:S(2)}, u32[]{:S(2)}) collective-permute-start(bf16[256,256]{1,0:T(8,128)(2,1)S(1)} %get-tuple-element.46), channel_id=1, source_target_pairs={{0,8},{8,16},{16,24},{24,32},{32,40},{40,48},{48,56},{56,64},{64,7... | collective-permute-start | bytes 393224 | tf_op jit(solution)/shard_map/ppermute | solution.py:410
  36.2 2.1 %collective-permute-start.8 = (bf16[256,256]{1,0:T(8,128)(2,1)S(1)}, bf16[256,256]{1,0:T(8,128)(2,1)S(1)}, u32[]{:S(2)}, u32[]{:S(2)}) collective-permute-start(bf16[256,256]{1,0:T(8,128)(2,1)S(1)} %get-tuple-element.47), channel_id=1, source_target_pairs={{8,0},{16,8},{24,16},{32,24},{40,32},{48,40},{56,48},{64,56},{72,6... | collective-permute-start | bytes 393224 | tf_op jit(solution)/shard_map/ppermute | solution.py:411
  38.3 4.3 %collective-permute-done.8.next_ref = bf16[256,256]{1,0:T(8,128)(2,1)S(1)} collective-permute-done((bf16[256,256]{1,0:T(8,128)(2,1)S(1)}, bf16[256,256]{1,0:T(8,128)(2,1)S(1)}, u32[]{:S(2)}, u32[]{:S(2)}) %collective-permute-start.8) | collective-permute-done | bytes 131104 | tf_op jit(solution)/shard_map/ppermute | solution.py:411
  42.6 4.3 %stats.1 = (f32[768,128]{1,0:T(8,128)S(1)}, f32[768,128]{1,0:T(8,128)S(1)}) custom-call(s32[5]{0:T(128)S(1)} %stack.23.place_ref.core_ref, bf16[256,256]{1,0:T(8,128)(2,1)S(1)} %collective-permute-done.7.prev_ref, bf16[256,256]{1,0:T(8,128)(2,1)S(1)} %collective-permute-done.8.next_ref, bf16[144,512]{1,0:T(8,128)(2,1)S(1)} %get-tuple-element.37.refs_0_, ...), custom_call_target="tpu_custom_call" | custom-call | tf_op jit(solution)/shard_map/stats/pallas_call | solution.py:35
  47.0 1.7 %collective-permute-done.9.got_ref = f32[768,128]{1,0:T(8,128)S(1)} collective-permute-done((f32[768,128]{1,0:T(8,128)S(1)}, f32[768,128]{1,0:T(8,128)S(1)}, u32[]{:S(2)}, u32[]{:S(2)}) %collective-permute-start.9) | collective-permute-done | bytes 393248 | tf_op jit(solution)/shard_map/ppermute | solution.py:426
  50.1 3.8 %collective-permute-start.11 = (f32[192,128]{1,0:T(8,128)S(1)}, f32[192,128]{1,0:T(8,128)S(1)}, u32[]{:S(2)}, u32[]{:S(2)}) collective-permute-start(f32[192,128]{1,0:T(8,128)S(1)} %get-tuple-element.51), channel_id=1, source_target_pairs={{0,32},{8,40},{16,48},{24,56},{32,0},{40,8},{48,16},{56,24},{64,96... | collective-permute-start | bytes 294920 | tf_op jit(solution)/shard_map/ppermute | solution.py:428
  54.0 1.9 %in_grad.1 = bf16[512,128]{1,0:T(8,128)(2,1)} custom-call(bf16[256,256]{1,0:T(8,128)(2,1)S(1)} %collective-permute-done.7.prev_ref, bf16[512,128]{1,0:T(8,128)(2,1)S(1)} %bitcast.10, bf16[256,256]{1,0:T(8,128)(2,1)S(1)} %collective-permute-done.8.next_ref, bf16[27,128,128]{2,1,0:T(8,128)(2,1)S(1)} %copy-done), custom_call_target="tpu_custom_call" | custom-call | tf_op jit(solution)/shard_map/in_grad/pallas_call | solution.py:35
  55.8 3.0 %collective-permute-done.11.refs_2_ = f32[192,128]{1,0:T(8,128)S(1)} collective-permute-done((f32[192,128]{1,0:T(8,128)S(1)}, f32[192,128]{1,0:T(8,128)S(1)}, u32[]{:S(2)}, u32[]{:S(2)}) %collective-permute-start.11) | collective-permute-done | bytes 98336 | tf_op jit(solution)/shard_map/ppermute | solution.py:428
  59.1 1.9 %collective-permute-start.14 = (f32[192,128]{1,0:T(8,128)S(1)}, f32[192,128]{1,0:T(8,128)S(1)}, u32[]{:S(2)}, u32[]{:S(2)}) collective-permute-start(f32[192,128]{1,0:T(8,128)S(1)} %fold_y.1.refs_0_), channel_id=1, source_target_pairs={{0,128},{8,136},{16,144},{24,152},{32,160},{40,168},{48,176},{56,1... | collective-permute-start | bytes 294920 | tf_op jit(solution)/shard_map/ppermute | solution.py:431
  62.6 6.6 %collective-permute-done.14.refs_2_ = f32[192,128]{1,0:T(8,128)S(1)} collective-permute-done((f32[192,128]{1,0:T(8,128)S(1)}, f32[192,128]{1,0:T(8,128)S(1)}, u32[]{:S(2)}, u32[]{:S(2)}) %collective-permute-start.14) | collective-permute-done | bytes 98336 | tf_op jit(solution)/shard_map/ppermute | solution.py:431
  69.8 3.0 %collective-permute-start.18 = (f32[192,128]{1,0:T(8,128)S(1)}, f32[192,128]{1,0:T(8,128)S(1)}, u32[]{:S(2)}, u32[]{:S(2)}) collective-permute-start(f32[192,128]{1,0:T(8,128)S(1)} %fold_z.1.refs_0_), channel_id=1, source_target_pairs={{0,48},{8,56},{16,0},{24,8},{32,16},{40,24},{48,32},{56,40},{64,11... | collective-permute-start | bytes 294920 | tf_op jit(solution)/shard_map/ppermute | solution.py:438
  73.5 1.9 %collective-permute-start.19 = (f32[192,128]{1,0:T(8,128)S(1)}, f32[192,128]{1,0:T(8,128)S(1)}, u32[]{:S(2)}, u32[]{:S(2)}) collective-permute-start(f32[192,128]{1,0:T(8,128)S(1)} %fold_z.1.refs_0_), channel_id=1, source_target_pairs={{0,8},{8,0},{16,24},{24,16},{32,40},{40,32},{48,56},{56,48},{64,72... | collective-permute-start | bytes 294920 | tf_op jit(solution)/shard_map/ppermute | solution.py:439
  75.4 2.6 %collective-permute-start.22 = (f32[192,128]{1,0:T(8,128)S(1)}, f32[192,128]{1,0:T(8,128)S(1)}, u32[]{:S(2)}, u32[]{:S(2)}) collective-permute-start(f32[192,128]{1,0:T(8,128)S(1)} %collective-permute-done.18.refs_3_), channel_id=1, source_target_pairs={{0,8},{8,0},{16,24},{24,16},{32,40},{40,32},{48,56},{56,48},{64,72... | collective-permute-start | bytes 294920 | tf_op jit(solution)/shard_map/ppermute | solution.py:439
  78.0 2.7 %collective-permute-start.21 = (f32[192,128]{1,0:T(8,128)S(1)}, f32[192,128]{1,0:T(8,128)S(1)}, u32[]{:S(2)}, u32[]{:S(2)}) collective-permute-start(f32[192,128]{1,0:T(8,128)S(1)} %collective-permute-done.17.refs_2_), channel_id=1, source_target_pairs={{0,8},{8,0},{16,24},{24,16},{32,40},{40,32},{48,56},{56,48},{64,72... | collective-permute-start | bytes 294920 | tf_op jit(solution)/shard_map/ppermute | solution.py:439
  82.6 24.3 %forward.1 = (f32[432,128]{1,0:T(8,128)S(1)}, f32[960,128]{1,0:T(8,128)S(1)}, f32[128,128]{1,0:T(8,128)S(1)}, f32[8,8,128]{2,1,0:T(8,128)}) custom-call(s32[5]{0:T(128)S(1)} %stack.23.place_ref.core_ref, f32[192,128]{1,0:T(8,128)S(1)} %fold_z.1.refs_0_, f32[192,128]{1,0:T(8,128)S(1)} %collective-permute-done.16.refs_1_, ...), custom_call_target="tpu_custom_call" | custom-call | tf_op jit(solution)/shard_map/forward/pallas_call | solution.py:35
  106.9 7.2 %all-to-all-start = ((f32[8,8,128]{2,1,0:T(8,128)}), f32[8,8,128]{2,1,0:T(8,128)S(1)}, u32[]{:S(2)}, u32[]{:S(2)}) async-start(f32[8,8,128]{2,1,0:T(8,128)} %get-tuple-element.61), calls=%async_computation | async-start | bytes 65536 | tf_op jit(solution)/shard_map/all_to_all | solution.py:447
  114.1 1.9 %backward.1.raw_ref = f32[432,128]{1,0:T(8,128)S(1)} custom-call(f32[432,128]{1,0:T(8,128)S(1)} %get-tuple-element.58.z_ref, f32[960,128]{1,0:T(8,128)S(1)} %get-tuple-element.59.y_ref, f32[128,128]{1,0:T(8,128)S(1)} %get-tuple-element.60.right_ref), custom_call_target="tpu_custom_call" | custom-call | tf_op jit(solution)/shard_map/backward/pallas_call | solution.py:35
  116.1 7.1 %all-to-all-done.parts_ref = f32[8,8,128]{2,1,0:T(8,128)S(1)} async-done(((f32[8,8,128]{2,1,0:T(8,128)}), f32[8,8,128]{2,1,0:T(8,128)S(1)}, u32[]{:S(2)}, u32[]{:S(2)}) %all-to-all-start) | async-done | bytes 32800 | tf_op jit(solution)/shard_map/all_to_all | solution.py:447
  (42 shorter events, 15.0 us)
Async XLA Ops:
  3.1 17.6 %collective-permute-start = (bf16[192,512]{1,0:T(8,128)(2,1)S(1)}, bf16[192,512]{1,0:T(8,128)(2,1)S(1)}, u32[]{:S(2)}, u32[]{:S(2)}) collective-permute-start(bf16[192,512]{1,0:T(8,128)(2,1)S(1)} %get-tuple-element.32), channel_id=1, source_target_pairs={{0,4},{1,5},{2,6},{3,7},{4,0},{5,1},{6,2},{7,3},{8,12},{9,13},{10,... | collective-permute-start | bytes 589832 | tf_op jit(solution)/shard_map/ppermute | solution.py:401
  11.0 5.6 %collective-permute-start.1 = (bf16[144,512]{1,0:T(8,128)(2,1)S(1)}, bf16[144,512]{1,0:T(8,128)(2,1)S(1)}, u32[]{:S(2)}, u32[]{:S(2)}) collective-permute-start(bf16[144,512]{1,0:T(8,128)(2,1)S(1)} %get-tuple-element.34), channel_id=1, source_target_pairs={{0,1},{1,2},{2,3},{3,0},{4,5},{5,6},{6,7},{7,4},{8,9},{9,10},{10,1... | collective-permute-start | bytes 442376 | tf_op jit(solution)/shard_map/ppermute | solution.py:402
  12.2 8.5 %collective-permute-start.2 = (bf16[144,512]{1,0:T(8,128)(2,1)S(1)}, bf16[144,512]{1,0:T(8,128)(2,1)S(1)}, u32[]{:S(2)}, u32[]{:S(2)}) collective-permute-start(bf16[144,512]{1,0:T(8,128)(2,1)S(1)} %get-tuple-element.35), channel_id=1, source_target_pairs={{0,2},{1,3},{2,0},{3,1},{4,6},{5,7},{6,4},{7,5},{8,10},{9,11},{10,... | collective-permute-start | bytes 442376 | tf_op jit(solution)/shard_map/ppermute | solution.py:402
  14.6 6.1 %collective-permute-start.3 = (bf16[144,512]{1,0:T(8,128)(2,1)S(1)}, bf16[144,512]{1,0:T(8,128)(2,1)S(1)}, u32[]{:S(2)}, u32[]{:S(2)}) collective-permute-start(bf16[144,512]{1,0:T(8,128)(2,1)S(1)} %get-tuple-element.36), channel_id=1, source_target_pairs={{0,3},{1,0},{2,1},{3,2},{4,7},{5,4},{6,5},{7,6},{8,11},{9,8},{10,9... | collective-permute-start | bytes 442376 | tf_op jit(solution)/shard_map/ppermute | solution.py:402
  21.3 5.3 %collective-permute-start.4 = (bf16[144,512]{1,0:T(8,128)(2,1)S(1)}, bf16[144,512]{1,0:T(8,128)(2,1)S(1)}, u32[]{:S(2)}, u32[]{:S(2)}) collective-permute-start(bf16[144,512]{1,0:T(8,128)(2,1)S(1)} %get-tuple-element.43), channel_id=1, source_target_pairs={{0,1},{1,2},{2,3},{3,0},{4,5},{5,6},{6,7},{7,4},{8,9},{9,10},{10,1... | collective-permute-start | bytes 442376 | tf_op jit(solution)/shard_map/ppermute | solution.py:406
  23.1 7.3 %collective-permute-start.5 = (bf16[144,512]{1,0:T(8,128)(2,1)S(1)}, bf16[144,512]{1,0:T(8,128)(2,1)S(1)}, u32[]{:S(2)}, u32[]{:S(2)}) collective-permute-start(bf16[144,512]{1,0:T(8,128)(2,1)S(1)} %get-tuple-element.44), channel_id=1, source_target_pairs={{0,2},{1,3},{2,0},{3,1},{4,6},{5,7},{6,4},{7,5},{8,10},{9,11},{10,... | collective-permute-start | bytes 442376 | tf_op jit(solution)/shard_map/ppermute | solution.py:406
  25.1 5.3 %collective-permute-start.6 = (bf16[144,512]{1,0:T(8,128)(2,1)S(1)}, bf16[144,512]{1,0:T(8,128)(2,1)S(1)}, u32[]{:S(2)}, u32[]{:S(2)}) collective-permute-start(bf16[144,512]{1,0:T(8,128)(2,1)S(1)} %get-tuple-element.45), channel_id=1, source_target_pairs={{0,3},{1,0},{2,1},{3,2},{4,7},{5,4},{6,5},{7,6},{8,11},{9,8},{10,9... | collective-permute-start | bytes 442376 | tf_op jit(solution)/shard_map/ppermute | solution.py:406
  30.4 7.8 %collective-permute-start.7 = (bf16[256,256]{1,0:T(8,128)(2,1)S(1)}, bf16[256,256]{1,0:T(8,128)(2,1)S(1)}, u32[]{:S(2)}, u32[]{:S(2)}) collective-permute-start(bf16[256,256]{1,0:T(8,128)(2,1)S(1)} %get-tuple-element.46), channel_id=1, source_target_pairs={{0,8},{8,16},{16,24},{24,32},{32,40},{40,48},{48,56},{56,64},{64,7... | collective-permute-start | bytes 393224 | tf_op jit(solution)/shard_map/ppermute | solution.py:410
  36.2 6.4 %collective-permute-start.8 = (bf16[256,256]{1,0:T(8,128)(2,1)S(1)}, bf16[256,256]{1,0:T(8,128)(2,1)S(1)}, u32[]{:S(2)}, u32[]{:S(2)}) collective-permute-start(bf16[256,256]{1,0:T(8,128)(2,1)S(1)} %get-tuple-element.47), channel_id=1, source_target_pairs={{8,0},{16,8},{24,16},{32,24},{40,32},{48,40},{56,48},{64,56},{72,6... | collective-permute-start | bytes 393224 | tf_op jit(solution)/shard_map/ppermute | solution.py:411
  46.9 1.8 %collective-permute-start.9 = (f32[768,128]{1,0:T(8,128)S(1)}, f32[768,128]{1,0:T(8,128)S(1)}, u32[]{:S(2)}, u32[]{:S(2)}) collective-permute-start(f32[768,128]{1,0:T(8,128)S(1)} %get-tuple-element.49), channel_id=1, source_target_pairs={{0,8},{8,0},{16,24},{24,16},{32,40},{40,32},{48,56},{56,48},{64,72... | collective-permute-start | bytes 1179656 | tf_op jit(solution)/shard_map/ppermute | solution.py:426
  48.7 7.1 %collective-permute-start.10 = (f32[192,128]{1,0:T(8,128)S(1)}, f32[192,128]{1,0:T(8,128)S(1)}, u32[]{:S(2)}, u32[]{:S(2)}) collective-permute-start(f32[192,128]{1,0:T(8,128)S(1)} %get-tuple-element.50), channel_id=1, source_target_pairs={{0,16},{8,24},{16,32},{24,40},{32,48},{40,56},{48,0},{56,8},{64,80... | collective-permute-start | bytes 294920 | tf_op jit(solution)/shard_map/ppermute | solution.py:428
  50.1 8.7 %collective-permute-start.11 = (f32[192,128]{1,0:T(8,128)S(1)}, f32[192,128]{1,0:T(8,128)S(1)}, u32[]{:S(2)}, u32[]{:S(2)}) collective-permute-start(f32[192,128]{1,0:T(8,128)S(1)} %get-tuple-element.51), channel_id=1, source_target_pairs={{0,32},{8,40},{16,48},{24,56},{32,0},{40,8},{48,16},{56,24},{64,96... | collective-permute-start | bytes 294920 | tf_op jit(solution)/shard_map/ppermute | solution.py:428
  54.0 4.9 %collective-permute-start.12 = (f32[192,128]{1,0:T(8,128)S(1)}, f32[192,128]{1,0:T(8,128)S(1)}, u32[]{:S(2)}, u32[]{:S(2)}) collective-permute-start(f32[192,128]{1,0:T(8,128)S(1)} %get-tuple-element.52), channel_id=1, source_target_pairs={{0,48},{8,56},{16,0},{24,8},{32,16},{40,24},{48,32},{56,40},{64,11... | collective-permute-start | bytes 294920 | tf_op jit(solution)/shard_map/ppermute | solution.py:428
  58.9 3.7 %collective-permute-start.15 = (f32[192,128]{1,0:T(8,128)S(1)}, f32[192,128]{1,0:T(8,128)S(1)}, u32[]{:S(2)}, u32[]{:S(2)}) collective-permute-start(f32[192,128]{1,0:T(8,128)S(1)} %fold_y.1.refs_0_), channel_id=1, source_target_pairs={{0,192},{8,200},{16,208},{24,216},{32,224},{40,232},{48,240},{56,2... | collective-permute-start | bytes 294920 | tf_op jit(solution)/shard_map/ppermute | solution.py:431
  59.1 10.0 %collective-permute-start.14 = (f32[192,128]{1,0:T(8,128)S(1)}, f32[192,128]{1,0:T(8,128)S(1)}, u32[]{:S(2)}, u32[]{:S(2)}) collective-permute-start(f32[192,128]{1,0:T(8,128)S(1)} %fold_y.1.refs_0_), channel_id=1, source_target_pairs={{0,128},{8,136},{16,144},{24,152},{32,160},{40,168},{48,176},{56,1... | collective-permute-start | bytes 294920 | tf_op jit(solution)/shard_map/ppermute | solution.py:431
  61.1 8.1 %collective-permute-start.13 = (f32[192,128]{1,0:T(8,128)S(1)}, f32[192,128]{1,0:T(8,128)S(1)}, u32[]{:S(2)}, u32[]{:S(2)}) collective-permute-start(f32[192,128]{1,0:T(8,128)S(1)} %fold_y.1.refs_0_), channel_id=1, source_target_pairs={{0,64},{8,72},{16,80},{24,88},{32,96},{40,104},{48,112},{56,120},{... | collective-permute-start | bytes 294920 | tf_op jit(solution)/shard_map/ppermute | solution.py:431
  69.8 5.6 %collective-permute-start.18 = (f32[192,128]{1,0:T(8,128)S(1)}, f32[192,128]{1,0:T(8,128)S(1)}, u32[]{:S(2)}, u32[]{:S(2)}) collective-permute-start(f32[192,128]{1,0:T(8,128)S(1)} %fold_z.1.refs_0_), channel_id=1, source_target_pairs={{0,48},{8,56},{16,0},{24,8},{32,16},{40,24},{48,32},{56,40},{64,11... | collective-permute-start | bytes 294920 | tf_op jit(solution)/shard_map/ppermute | solution.py:438
  72.8 5.2 %collective-permute-start.17 = (f32[192,128]{1,0:T(8,128)S(1)}, f32[192,128]{1,0:T(8,128)S(1)}, u32[]{:S(2)}, u32[]{:S(2)}) collective-permute-start(f32[192,128]{1,0:T(8,128)S(1)} %fold_z.1.refs_0_), channel_id=1, source_target_pairs={{0,32},{8,40},{16,48},{24,56},{32,0},{40,8},{48,16},{56,24},{64,96... | collective-permute-start | bytes 294920 | tf_op jit(solution)/shard_map/ppermute | solution.py:438
  73.3 7.3 %collective-permute-start.16 = (f32[192,128]{1,0:T(8,128)S(1)}, f32[192,128]{1,0:T(8,128)S(1)}, u32[]{:S(2)}, u32[]{:S(2)}) collective-permute-start(f32[192,128]{1,0:T(8,128)S(1)} %fold_z.1.refs_0_), channel_id=1, source_target_pairs={{0,16},{8,24},{16,32},{24,40},{32,48},{40,56},{48,0},{56,8},{64,80... | collective-permute-start | bytes 294920 | tf_op jit(solution)/shard_map/ppermute | solution.py:438
  73.5 8.1 %collective-permute-start.19 = (f32[192,128]{1,0:T(8,128)S(1)}, f32[192,128]{1,0:T(8,128)S(1)}, u32[]{:S(2)}, u32[]{:S(2)}) collective-permute-start(f32[192,128]{1,0:T(8,128)S(1)} %fold_z.1.refs_0_), channel_id=1, source_target_pairs={{0,8},{8,0},{16,24},{24,16},{32,40},{40,32},{48,56},{56,48},{64,72... | collective-permute-start | bytes 294920 | tf_op jit(solution)/shard_map/ppermute | solution.py:439
  75.4 6.3 %collective-permute-start.22 = (f32[192,128]{1,0:T(8,128)S(1)}, f32[192,128]{1,0:T(8,128)S(1)}, u32[]{:S(2)}, u32[]{:S(2)}) collective-permute-start(f32[192,128]{1,0:T(8,128)S(1)} %collective-permute-done.18.refs_3_), channel_id=1, source_target_pairs={{0,8},{8,0},{16,24},{24,16},{32,40},{40,32},{48,56},{56,48},{64,72... | collective-permute-start | bytes 294920 | tf_op jit(solution)/shard_map/ppermute | solution.py:439
  78.0 3.7 %collective-permute-start.21 = (f32[192,128]{1,0:T(8,128)S(1)}, f32[192,128]{1,0:T(8,128)S(1)}, u32[]{:S(2)}, u32[]{:S(2)}) collective-permute-start(f32[192,128]{1,0:T(8,128)S(1)} %collective-permute-done.17.refs_2_), channel_id=1, source_target_pairs={{0,8},{8,0},{16,24},{24,16},{32,40},{40,32},{48,56},{56,48},{64,72... | collective-permute-start | bytes 294920 | tf_op jit(solution)/shard_map/ppermute | solution.py:439
  80.7 1.9 %collective-permute-start.20 = (f32[192,128]{1,0:T(8,128)S(1)}, f32[192,128]{1,0:T(8,128)S(1)}, u32[]{:S(2)}, u32[]{:S(2)}) collective-permute-start(f32[192,128]{1,0:T(8,128)S(1)} %collective-permute-done.16.refs_1_), channel_id=1, source_target_pairs={{0,8},{8,0},{16,24},{24,16},{32,40},{40,32},{48,56},{56,48},{64,72... | collective-permute-start | bytes 294920 | tf_op jit(solution)/shard_map/ppermute | solution.py:439
  106.9 16.3 %all-to-all-start = ((f32[8,8,128]{2,1,0:T(8,128)}), f32[8,8,128]{2,1,0:T(8,128)S(1)}, u32[]{:S(2)}, u32[]{:S(2)}) async-start(f32[8,8,128]{2,1,0:T(8,128)} %get-tuple-element.61), calls=%async_computation | async-start | bytes 65536 | tf_op jit(solution)/shard_map/all_to_all | solution.py:447
  (3 other events, 19.6 us)
